TPU v7x, 32 devices: a whole 2x2x4 slice. The times are simulated.
32 devices in a mesh: dp: 8 (over z, y), tensor: 4 (over x, core).
Axes of the slice: x: 2, y: 2, z: 4, core: 2. Of those that a mesh axis runs over, the one named last changes fastest.
Arguments:
- features: bfloat16 [128, 32, 256], P('dp', None, 'tensor'), may hold values from -6 to 6
- domain_index: int32 [4], replicated, may hold values from 0 to 1, as said below
- conv_first: bfloat16 [3, 3, 256, 512], P(None, None, None, 'tensor'), may hold values from -0.125 to 0.125
- conv_second: bfloat16 [3, 3, 512, 512], P(None, None, None, 'tensor'), may hold values from -0.09375 to 0.09375
- conv_third: bfloat16 [3, 3, 512, 512], P(None, None, None, 'tensor'), may hold values from -0.09375 to 0.09375
- shared_gain: float32 [3, 2, 512], P(None, None, 'tensor'), may hold values from 0.1 to 1.9
- shared_bias: float32 [3, 2, 512], P(None, None, 'tensor'), may hold values from -3 to 3
- mask_down: bfloat16 [3, 512, 512], P(None, None, 'tensor'), may hold values from -0.25 to 0.25
- mask_up: bfloat16 [3, 512, 512], P(None, None, 'tensor'), may hold values from -0.25 to 0.25
- task_conv: bfloat16 [3, 3, 3, 512, 512], P(None, None, None, None, 'tensor'), may hold values from -0.09375 to 0.09375
- task_gain: float32 [3, 3, 2, 512], P(None, None, None, 'tensor'), may hold values from 0.1 to 1.9
- task_bias: float32 [3, 3, 2, 512], P(None, None, None, 'tensor'), may hold values from -3 to 3
- shared_cotangent: bfloat16 [64, 16, 512], P('dp', None, 'tensor'), may hold values from -6 to 6
- task_cotangent: bfloat16 [3, 64, 16, 512], P(None, 'dp', None, 'tensor'), may hold values from -6 to 6
Outputs:
- shared_pooled: bfloat16 [64, 16, 512], P('dp', None, 'tensor')
- task_pooled: bfloat16 [3, 64, 16, 512], P(None, 'dp', None, 'tensor')
- features_grad: bfloat16 [128, 32, 256], P('dp', None, 'tensor')
- conv_first_grad: float32 [3, 3, 256, 512], P(None, None, None, 'tensor')
- conv_second_grad: float32 [3, 3, 512, 512], P(None, None, None, 'tensor')
- conv_third_grad: float32 [3, 3, 512, 512], P(None, None, None, 'tensor')
- shared_gain_grad: float32 [3, 2, 512], P(None, None, 'tensor')
- shared_bias_grad: float32 [3, 2, 512], P(None, None, 'tensor')
- mask_down_grad: float32 [3, 512, 512], P(None, None, 'tensor')
- mask_up_grad: float32 [3, 512, 512], P(None, None, 'tensor')
- task_conv_grad: float32 [3, 3, 3, 512, 512], P(None, None, None, None, 'tensor')
- task_gain_grad: float32 [3, 3, 2, 512], P(None, None, None, 'tensor')
- task_bias_grad: float32 [3, 3, 2, 512], P(None, None, None, 'tensor')
Inputs may be any that keep to these rules, and one draw needn't show every extreme that they name: `domain_index`: exactly 2 images belong to domain 0 and the others to domain 1.
All inputs are finite; a program needn't handle non-finite values.
Results may differ from a plain program's by a relative error of at most 0.025.
Values may be sent and summed in bfloat16 or wider, within the bound.
A program may use at most 128 MiB of HBM per device.

v0:
```python
import functools
import types

import jax
import jax.numpy as jnp
from jax import lax
from jax.experimental import pallas as pl
from jax.experimental.pallas import tpu as pltpu
from jax.sharding import PartitionSpec as P

DOMAINS = 2
TASKS = 3
H = 32
W = 32
ROWS = 16
PX = ROWS * W
IMAGE = H * W
LANES = 128
EPSILON = 1e-05
PIECES = 19
CHUNKS = (38, 36)
CHAINS = (
    (0, (18, 18), 2, True),
    (18, (8, 8), 2, True),
    (26, (8, 8), 2, True),
    (34, (4, 2), 0, False),
)
BOTH = (4, 2, 2, 0)
LAG = 2
ROUNDS = 19
WIDE = (2, 15, 16)
F32 = jnp.float32
BF16 = jnp.bfloat16
MESH = pl.DeviceIdType.MESH

FIRST, SECOND, THIRD, PROJ, LOGIT, MIXED = 0, 1, 2, 3, 6, 9


def dot(a, b):
    return lax.dot_general(a, b, (((1,), (0,)), ((), ())), preferred_element_type=F32)


def dot_nt(a, b):
    return lax.dot_general(a, b, (((1,), (1,)), ((), ())), preferred_element_type=F32)


def dot_tn(a, b):
    return lax.dot_general(a, b, (((0,), (0,)), ((), ())), preferred_element_type=F32)


def fold(values):
    return jnp.sum(values.reshape(values.shape[0] // 8, 8, LANES), axis=0)


def total(values):
    return jnp.sum(values, axis=0, keepdims=True)


def sigmoid(values):
    return 0.5 + 0.5 * jnp.tanh(0.5 * values)


def column(rows):
    return lax.broadcasted_iota(jnp.int32, (rows, LANES), 0) & (W - 1)


def from_left(values):
    rows = values.shape[0]
    return jnp.where(column(rows) == 0, 0.0, pltpu.roll(values, 1, 0))


def from_right(values):
    rows = values.shape[0]
    return jnp.where(column(rows) == W - 1, 0.0, pltpu.roll(values, rows - 1, 0))


def e_slot(layer):
    places = {THIRD: 6, SECOND: 3, FIRST: 4}
    return places[layer] if layer in places else (layer - 3) % 3 + (3 if LOGIT <= layer < MIXED else 0)


def loop(count, size, step, init=None):
    def run(index, carry):
        result = step(pl.multiple_of(index * size, size), carry)
        return carry if init is None else result

    return lax.fori_loop(0, count, run, 0 if init is None else init)


def kernel(dp_size, names, *refs):
    r = types.SimpleNamespace(**dict(zip(names, refs)))
    images = dp_size // 2
    d = lax.axis_index("dp")
    t = lax.axis_index("tensor")
    half = lax.rem(d, 2)
    image = lax.div(d, 2)
    core = lax.rem(t, 2)
    pair = lax.div(t, 2)
    partner = d + 1 - 2 * half
    peers = (t, t + 1 - 2 * core, t + 2 - 4 * pair, 3 - t)
    mate = (d, peers[1])
    across = (d, peers[2])
    beside = (partner, t)
    pending = {}

    def send(src, dst, send_sem, recv_sem, device):
        pltpu.make_async_remote_copy(
            src_ref=src,
            dst_ref=dst,
            send_sem=send_sem,
            recv_sem=recv_sem,
            device_id=device,
            device_id_type=MESH,
        ).start()

    def arrived(like, sem):
        pltpu.make_async_remote_copy(
            src_ref=like,
            dst_ref=like,
            send_sem=sem,
            recv_sem=sem,
            device_id=mate,
            device_id_type=MESH,
        ).wait_recv()

    def left(like, sem):
        pltpu.make_async_remote_copy(
            src_ref=like,
            dst_ref=like,
            send_sem=sem,
            recv_sem=sem,
            device_id=mate,
            device_id_type=MESH,
        ).wait_send()

    def sent_later(like, sem, key=None):
        pending.setdefault(key, []).append(lambda: left(like, sem))

    def flush(key):
        for wait in pending.pop(key, []):
            wait()

    def local(src, dst, sem):
        pltpu.make_async_copy(src, dst, sem).start()

    def emit(src, dst, index):
        local(src, dst, r.emit_sem.at[index])
        pending.setdefault(None, []).append(lambda: local_done(src, r.emit_sem.at[index]))

    def local_done(like, sem):
        pltpu.make_async_copy(like, like, sem).wait()

    for buffer in (r.x1, r.x2, r.x3, r.xm.at[0], r.xm.at[1], r.xm.at[2]):
        zero = jnp.zeros((W, buffer.shape[1]), BF16)
        buffer[0:W, :] = zero
        buffer[W + PX : 2 * W + PX, :] = zero
    zero = jnp.zeros((W, LANES), BF16)
    for index in range(6):
        for b in range(3):
            r.g3[index, b, 0:W, :] = zero
            r.g3[index, b, W + IMAGE : 2 * W + IMAGE, :] = zero
    for index in range(len(WIDE)):
        r.st8[index] = jnp.zeros((8, LANES), F32)

    barrier = pltpu.get_barrier_semaphore()

    def greet(step, carry):
        pl.semaphore_signal(
            barrier, inc=1, device_id=(lax.rem(d + step, dp_size), t), device_id_type=MESH
        )
        return carry

    lax.fori_loop(1, dp_size, greet, 0)
    for j in range(1, 4):
        for row in (d, partner):
            pl.semaphore_signal(barrier, inc=1, device_id=(row, peers[j]), device_id_type=MESH)
    local(r.feat, r.fm.at[0], r.weight_sem.at[6])
    small = ((r.sct, r.b_sct), (r.tct, r.b_tct), (r.sg, r.b_sg), (r.sb, r.b_sb), (r.tg, r.b_tg), (r.tb, r.b_tb))
    for index, (source, target) in enumerate(small):
        local(source, target, r.small_sem.at[index])
    for j in range(2):
        block = pair if j == 0 else 1 - pair
        rows = pl.ds(pl.multiple_of(block * LANES, LANES), LANES)
        local(
            r.k1.at[:, rows, :],
            r.w1.at[:, j * LANES : (j + 1) * LANES, :],
            r.weight_sem.at[5],
        )
    for index, (source, target) in enumerate(
        ((r.k2, r.w2), (r.k3, r.w3), (r.kt, r.wt), (r.md, r.wd), (r.mu, r.wu))
    ):
        for j in range(4):
            rows = pl.ds(pl.multiple_of(peers[j] * LANES, LANES), LANES)
            local(
                source.at[:, rows, :],
                target.at[:, j * LANES : (j + 1) * LANES, :],
                r.weight_sem.at[index],
            )
    pl.semaphore_wait(barrier, dp_size - 1 + 6)

    own_rows = pl.ds(W, PX)
    edge_from = pl.ds(pl.multiple_of(PX - half * (PX - W), W), W)
    edge_to = pl.ds(pl.multiple_of((W + PX) * half, W), W)
    edge_in = pl.ds(pl.multiple_of((W + PX) * (1 - half), W), W)
    core_lanes = pl.ds(pl.multiple_of(core * LANES, LANES), LANES)
    mate_lanes = pl.ds(pl.multiple_of((1 - core) * LANES, LANES), LANES)
    my_image_rows = pl.ds(pl.multiple_of(half * PX, PX), PX)
    other_image_rows = pl.ds(pl.multiple_of((1 - half) * PX, PX), PX)

    source_edge = pl.ds(pl.multiple_of((1 - half) * (PX - W), W), W)
    for j in range(4):
        send(
            r.feat.at[source_edge, :],
            r.fh.at[j],
            r.feat_send.at[0],
            r.feat_recv.at[0],
            (partner, peers[j]),
        )
    sent_later(r.fh, r.feat_send.at[0])
    for j in (2, 3, 1):
        send(r.feat, r.fm.at[j], r.feat_send.at[j], r.feat_recv.at[j], (d, peers[j]))
        sent_later(r.fm.at[j], r.feat_send.at[j])

    def unpool(ct, target):
        def step(start, carry):
            p = lax.broadcasted_iota(jnp.int32, (LANES, LANES), 0) + start
            q = lax.broadcasted_iota(jnp.int32, (LANES, LANES), 1)
            block = (p >> 6) * (W // 2) + ((p & (W - 1)) >> 1)
            pick = jnp.where(block == q, 0.25, 0.0).astype(BF16)
            target[pl.ds(start, LANES), :] = dot(pick, ct)

        loop(4, LANES, step)

    local_done(r.b_sct, r.small_sem.at[0])
    local_done(r.b_tct, r.small_sem.at[1])
    for task in range(TASKS):
        unpool(r.b_tct[task], r.e.at[e_slot(MIXED + task)])
    unpool(r.b_sct[...], r.e.at[e_slot(THIRD)])

    def joined(pieces, block):
        low, high = pieces[2 * block].astype(F32), pieces[2 * block + 1].astype(F32)
        first, last = jnp.where(core == 0, low, high), jnp.where(core == 0, high, low)
        return jnp.concatenate([first, last], axis=1).astype(BF16)

    def gather(buffer, inst, halo, base):
        own = buffer.at[pl.ds(base, PX), 0:LANES]
        if halo:
            for j in range(4):
                send(
                    buffer.at[edge_from, 0:LANES],
                    buffer.at[edge_to, j * LANES : (j + 1) * LANES],
                    r.g_send.at[inst, 3],
                    r.g_recv.at[inst, 3 + j // 2],
                    (partner, peers[j]),
                )
            sent_later(buffer.at[edge_from, :], r.g_send.at[inst, 3], inst)
        send(
            own,
            buffer.at[pl.ds(base, PX), 2 * LANES : 3 * LANES],
            r.g_send.at[inst, 1],
            r.g_recv.at[inst, 1],
            across,
        )
        send(
            own,
            buffer.at[pl.ds(base, PX), LANES : 2 * LANES],
            r.g_send.at[inst, 0],
            r.g_recv.at[inst, 0],
            mate,
        )
        sent_later(own, r.g_send.at[inst, 0], inst)
        sent_later(own, r.g_send.at[inst, 1], inst)

    def gather_forward(buffer, inst, base):
        crossed = buffer.at[pl.ds(base, PX), 2 * LANES : 3 * LANES]
        arrived(crossed, r.g_recv.at[inst, 1])
        send(
            crossed,
            buffer.at[pl.ds(base, PX), 3 * LANES : 4 * LANES],
            r.g_send.at[inst, 2],
            r.g_recv.at[inst, 2],
            mate,
        )
        sent_later(crossed, r.g_send.at[inst, 2], inst)

    def gather_near(buffer, inst, halo, base):
        arrived(buffer.at[pl.ds(base, PX), LANES : 2 * LANES], r.g_recv.at[inst, 0])
        if halo:
            arrived(buffer.at[edge_in, 0 : 2 * LANES], r.g_recv.at[inst, 3])

    def gather_far(buffer, inst, halo, base):
        if halo:
            arrived(buffer.at[edge_in, 2 * LANES : 4 * LANES], r.g_recv.at[inst, 4])
        arrived(buffer.at[pl.ds(base, PX), 3 * LANES : 4 * LANES], r.g_recv.at[inst, 2])

    def keep_input(buffer, target, inst, base):
        rows = pl.ds(base, PX)
        for q in range(2):
            block = 2 * half + lax.rem(q + core, 2)
            lanes = pl.ds(pl.multiple_of(block * LANES, LANES), LANES)
            local(
                buffer.at[rows, lanes],
                target.at[my_image_rows, q * LANES : (q + 1) * LANES],
                r.v_local.at[inst],
            )

    def exchange_input(buffer, target, inst, base):
        rows = pl.ds(base, PX)
        lanes = pl.ds(pl.multiple_of(2 * (1 - half) * LANES, LANES), LANES)
        src = buffer.at[rows, lanes]
        dst = target.at[my_image_rows, core_lanes]
        send(src, dst, r.v_send.at[inst, 0], r.v_recv.at[inst, 0], beside)
        sent_later(dst, r.v_send.at[inst, 0], 0 if inst == 1 else None)

    def forward_input(target, inst):
        piece = target.at[other_image_rows, core_lanes]
        arrived(piece, r.v_recv.at[inst, 0])
        send(piece, piece, r.v_send.at[inst, 1], r.v_recv.at[inst, 1], mate)
        sent_later(piece, r.v_send.at[inst, 1])

    def input_ready(target, inst):
        local_done(target.at[my_image_rows, :], r.v_local.at[inst])
        arrived(target.at[other_image_rows, mate_lanes], r.v_recv.at[inst, 1])

    def others(step, init):
        if dp_size > 8:
            return lax.fori_loop(1, dp_size, step, init)
        for offset in range(1, dp_size):
            init = step(offset, init)
        return init

    def sums_refs(index):
        if index in WIDE:
            return r.st8.at[WIDE.index(index)], r.sr8.at[WIDE.index(index)]
        return r.st.at[index], r.sr.at[index]

    def sums_send(index, rows):
        mine, theirs = sums_refs(index)
        for at, row in enumerate(rows):
            mine[at : at + 1, :] = row

        def step(offset, carry):
            send(
                mine,
                theirs.at[offset - 1],
                r.st_send.at[index],
                r.st_recv.at[index],
                (lax.rem(d + offset, dp_size), t),
            )
            return carry

        others(step, 0)
        sent_later(theirs, r.st_send.at[index])

    def sums_same(index):
        mine, theirs = sums_refs(index)
        arrived(theirs, r.st_recv.at[index])

        def step(offset, same):
            return same + r.same[pl.ds(offset, 1), :] * theirs[offset - 1]

        return others(step, mine[...])

    def sums_recv(index):
        same = sums_same(index)
        mine, theirs = sums_refs(index)

        def step(offset, other):
            return other + (1.0 - r.same[pl.ds(offset, 1), :]) * theirs[offset - 1]

        return same, others(step, jnp.zeros(mine.shape, F32))

    zeros8 = jnp.zeros((8, LANES), F32)
    domain = r.dom[image]
    my_domain = jnp.full((1, LANES), domain.astype(F32))
    members = lax.fori_loop(
        0, images, lambda i, n: n + jnp.where(r.dom[i] == domain, 1.0, 0.0), jnp.float32(0)
    )
    inverse_count = 1.0 / (jnp.full((1, LANES), members) * IMAGE)

    def mark(offset, carry):
        source = lax.div(lax.rem(d - offset + dp_size, dp_size), 2)
        weight = jnp.where(r.dom[source] == domain, 1.0, 0.0)
        r.same[pl.ds(offset, 1), :] = jnp.full((1, LANES), weight)
        return carry

    lax.fori_loop(1, dp_size, mark, 0)

    def choose(table, row):
        return table[row, 0:1, :] * (1.0 - my_domain) + table[row, 1:2, :] * my_domain

    def norm_setup(layer, sums, at):
        center = sums[2 * at : 2 * at + 1, :] * inverse_count
        square = sums[2 * at + 1 : 2 * at + 2, :] * inverse_count
        invstd = lax.rsqrt(square - center * center + EPSILON)
        if layer < 3:
            gain, bias = choose(r.b_sg, layer), choose(r.b_sb, layer)
        else:
            gain, bias = choose(r.b_tg, layer - 3), choose(r.b_tb, layer - 3)
        scale = gain * invstd
        r.bn[layer, 0:1, :] = center
        r.bn[layer, 1:2, :] = invstd
        r.bn[layer, 2:3, :] = scale
        r.bn[layer, 3:4, :] = bias - center * scale

    def pre_activation(layer, start):
        return r.pre[layer, pl.ds(start, LANES), :] * r.bn[layer, 2:3, :] + r.bn[layer, 3:4, :]

    def normed(layer, start):
        return (r.pre[layer, pl.ds(start, LANES), :] - r.bn[layer, 0:1, :]) * r.bn[layer, 1:2, :]

    def silu_to(layer, target, base):
        def step(start, carry):
            z = pre_activation(layer, start)
            target[pl.ds(base + start, LANES), 0:LANES] = (z * sigmoid(z)).astype(BF16)

        loop(4, LANES, step)

    def conv_part(buffer, weight, low, high):
        windows = [buffer[a * W : a * W + PX, low:high] for a in range(3)]
        taps = [
            jnp.concatenate([weight[3 * a + b, low:high, :] for b in range(3)], axis=1)
            for a in range(3)
        ]
        return dot(jnp.concatenate(windows, axis=1), jnp.concatenate(taps, axis=0))

    def conv_own(buffer, weight, width, acc_ref):
        acc_ref[...] = conv_part(buffer, weight, 0, width)

    def conv(buffer, weight, layer, width, acc_ref):
        acc_ref[...] += conv_part(buffer, weight, width, 2 * width)

        def step(start, carry):
            rows = pl.ds(start, LANES)
            out = (
                acc_ref[rows, LANES : 2 * LANES]
                + from_left(acc_ref[rows, 0:LANES])
                + from_right(acc_ref[rows, 2 * LANES :])
            )
            r.pre[layer, rows, :] = out
            return (carry[0] + fold(out), carry[1] + fold(out * out))

        sums = loop(4, LANES, step, (zeros8, zeros8))
        return [total(sums[0]), total(sums[1])]

    def column_sums(layer):
        def step(start, carry):
            out = r.pre[layer, pl.ds(start, LANES), :]
            return (carry[0] + fold(out), carry[1] + fold(out * out))

        sums = loop(4, LANES, step, (zeros8, zeros8))
        return [total(sums[0]), total(sums[1])]

    def pool(source, store):
        pairs = source[pl.ds(0, PX // 2, stride=2), :] + source[pl.ds(1, PX // 2, stride=2), :]
        blocks = jnp.sum(pairs.reshape(ROWS // 2, 2, W // 2, LANES), axis=1)
        store((0.25 * blocks).reshape(PX // 4, LANES).astype(BF16))

    local_done(r.fm.at[0], r.weight_sem.at[6])
    arrived(r.fm.at[1], r.feat_recv.at[1])
    r.x1[W : W + PX, 0:LANES] = joined([r.fm[0], r.fm[1]], 0)
    arrived(r.fh, r.feat_recv.at[0])
    edges = [r.fh[j] for j in range(4)]
    for block in range(2):
        r.x1[edge_in, block * LANES : (block + 1) * LANES] = joined(edges, block)
    local_done(r.w1, r.weight_sem.at[5])
    conv_own(r.x1, r.w1, LANES, r.acc.at[0])
    arrived(r.fm.at[2], r.feat_recv.at[2])
    arrived(r.fm.at[3], r.feat_recv.at[3])
    r.x1[W : W + PX, LANES : 2 * LANES] = joined([r.fm[2], r.fm[3]], 0)
    lanes = pl.ds(pl.multiple_of(half * LANES, LANES), LANES)
    local(r.x1.at[own_rows, lanes], r.v1.at[my_image_rows, :], r.v_local.at[0])
    lanes = pl.ds(pl.multiple_of((1 - half) * LANES, LANES), LANES)
    piece = r.v1.at[pl.ds(pl.multiple_of(half * PX + core * 256, 256), 256), :]
    send(
        r.x1.at[pl.ds(pl.multiple_of(W + core * 256, W), 256), lanes],
        piece,
        r.v_send.at[0, 0],
        r.v_recv.at[0, 0],
        beside,
    )
    sent_later(piece, r.v_send.at[0, 0])
    sums_send(0, conv(r.x1, r.w1, FIRST, LANES, r.acc.at[0]))
    local_done(r.w2, r.weight_sem.at[0])
    local_done(r.w3, r.weight_sem.at[1])
    local_done(r.wt, r.weight_sem.at[2])
    local_done(r.wd, r.weight_sem.at[3])
    local_done(r.wu, r.weight_sem.at[4])
    for index in range(2, 6):
        local_done(small[index][1], r.small_sem.at[index])
    same = sums_same(0)
    norm_setup(FIRST, same, 0)
    silu_to(FIRST, r.x2, W)
    gather(r.x2, 0, True, W)
    gather_near(r.x2, 0, True, W)
    conv_own(r.x2, r.w2, 256, r.acc.at[0])
    gather_forward(r.x2, 0, W)
    exchange_input(r.x2, r.v2, 1, W)
    piece = r.v1.at[pl.ds(pl.multiple_of((1 - half) * PX + core * 256, 256), 256), :]
    arrived(piece, r.v_recv.at[0, 0])
    send(piece, piece, r.v_send.at[0, 1], r.v_recv.at[0, 1], mate)
    sent_later(piece, r.v_send.at[0, 1])
    gather_far(r.x2, 0, True, W)
    keep_input(r.x2, r.v2, 1, W)

    sums_send(1, conv(r.x2, r.w2, SECOND, 256, r.acc.at[0]))

    taps = jnp.concatenate([r.wd[task] for task in range(TASKS)], axis=1)
    out = dot(r.x2[W : W + PX, :], taps)
    for task in range(TASKS):
        r.pre[PROJ + task] = out[:, task * LANES : (task + 1) * LANES]
    rows6 = []
    for task in range(TASKS):
        rows6 += column_sums(PROJ + task)
    sums_send(2, rows6)
    same = sums_same(1)
    norm_setup(SECOND, same, 0)
    silu_to(SECOND, r.x3, W)
    gather(r.x3, 1, True, W)
    same = sums_same(2)
    for task in range(TASKS):
        norm_setup(PROJ + task, same, task)
        silu_to(PROJ + task, r.xa.at[task], 0)
    def third_own():
        gather_near(r.x3, 1, True, W)
        conv_own(r.x3, r.w3, 256, r.acc.at[0])

    def activated_out():
        for task in range(TASKS):
            gather(r.xa.at[task], 2 + task, False, 0)

    def third_forward():
        gather_forward(r.x3, 1, W)
        exchange_input(r.x3, r.v3, 2, W)

    def third_far():
        gather_far(r.x3, 1, True, W)
        keep_input(r.x3, r.v3, 2, W)
        sums_send(3, conv(r.x3, r.w3, THIRD, 256, r.acc.at[0]))

    def turn_second():
        input_ready(r.v2, 1)
        r.vt[0] = r.v2[...].T

    def shared_pool():
        def store_shared(value):
            r.b_sp[...] = value

        pool(r.h3, store_shared)
        emit(r.b_sp, r.osp, 0)

    def logits(task):
        gather_near(r.xa.at[task], 2 + task, False, 0)
        gather_far(r.xa.at[task], 2 + task, False, 0)

        r.pre[LOGIT + task] = dot(r.xa[task], r.wu[task])
        sums_send(4 + task, column_sums(LOGIT + task))

    def attend(task):
        norm_setup(LOGIT + task, sums_same(4 + task), 0)

        def step(start, carry):
            attention = sigmoid(pre_activation(LOGIT + task, start))
            r.att[task, pl.ds(start, LANES), :] = attention
            r.xm[task, pl.ds(start + W, LANES), 0:LANES] = (
                attention * r.h3[pl.ds(start, LANES), :]
            ).astype(BF16)

        loop(4, LANES, step)
        gather(r.xm.at[task], 5 + task, True, W)

    def activate():
        norm_setup(THIRD, sums_same(3), 0)

        def step(start, carry):
            z = pre_activation(THIRD, start)
            r.h3[pl.ds(start, LANES), :] = z * sigmoid(z)

        loop(4, LANES, step)

    def turn_activated(task):
        flush(2 + task)
        r.xa[task] = r.xa[task].T

    def mixed_own(task):
        gather_near(r.xm.at[task], 5 + task, True, W)
        conv_own(r.xm.at[task], r.wt.at[pl.ds(9 * task, 9)], 256, r.acc.at[task % 2])

    def mixed_forward(task):
        gather_forward(r.xm.at[task], 5 + task, W)
        exchange_input(r.xm.at[task], r.vm.at[task], 3 + task, W)

    def mixed_far(task):
        gather_far(r.xm.at[task], 5 + task, True, W)
        keep_input(r.xm.at[task], r.vm.at[task], 3 + task, W)
        weight = r.wt.at[pl.ds(9 * task, 9)]
        sums_send(7 + task, conv(r.xm.at[task], weight, MIXED + task, 256, r.acc.at[task % 2]))

    def mixed_slope(task):
        layer = MIXED + task
        norm_setup(layer, sums_same(7 + task), 0)

        def step(start, carry):
            z = pre_activation(layer, start)
            q = sigmoid(z)
            r.ht[task, pl.ds(start, LANES), :] = z * q
            e = r.e[e_slot(layer), pl.ds(start, LANES), :] * (q * (1.0 + z * (1.0 - q)))
            r.e[e_slot(layer), pl.ds(start, LANES), :] = e
            return (carry[0] + fold(e * normed(layer, start)), carry[1] + fold(e))

        sums = loop(4, LANES, step, (zeros8, zeros8))
        sums_send(10 + task, [total(sums[0]), total(sums[1])])

    def mixed_pool(task):
        def store_task(value):
            r.b_tp[task] = value

        pool(r.ht.at[task], store_task)

    def slope_sums(layer, upstream):
        def step(start, carry):
            z = pre_activation(layer, start)
            q = sigmoid(z)
            e = upstream(start) * (q * (1.0 + z * (1.0 - q)))
            r.e[e_slot(layer), pl.ds(start, LANES), :] = e
            return (carry[0] + fold(e * normed(layer, start)), carry[1] + fold(e))

        sums = loop(4, LANES, step, (zeros8, zeros8))
        return [total(sums[0]), total(sums[1])]

    def store_gains(gain_at, bias_at, same, other, at):
        for target, row in ((gain_at, 2 * at), (bias_at, 2 * at + 1)):
            mine, rest = same[row : row + 1, :], other[row : row + 1, :]
            r.b_gb[target : target + 1, :] = mine * (1.0 - my_domain) + rest * my_domain
            r.b_gb[target + 1 : target + 2, :] = mine * my_domain + rest * (1.0 - my_domain)

    def store_layer_gains(layer, same, other, at):
        if layer < 3:
            store_gains(2 * layer, 6 + 2 * layer, same, other, at)
        else:
            store_gains(12 + 2 * (layer - 3), 30 + 2 * (layer - 3), same, other, at)

    def grad_tile(layer, start, sums, at):
        e = r.e[e_slot(layer), pl.ds(start, LANES), :]
        gain_sum = sums[2 * at : 2 * at + 1, :]
        bias_sum = sums[2 * at + 1 : 2 * at + 2, :]
        return r.bn[layer, 2:3, :] * (
            e - (bias_sum + normed(layer, start) * gain_sum) * inverse_count
        )

    def shifted(inst, start, rows, values):
        r.g3[inst, 0, pl.ds(start, rows), :] = from_right(values).astype(BF16)
        r.g3[inst, 2, pl.ds(start, rows), :] = from_left(values).astype(BF16)

    grad_edge = pl.ds(pl.multiple_of(PX + W * half, W), W)
    grad_edge_in = pl.multiple_of(PX + W * (1 - half), W)
    grad_rest = pl.ds(pl.multiple_of(W + (PX + W) * half, W), PX - W)
    grad_rest_in = pl.multiple_of(W + (PX + W) * (1 - half), W)

    def conv_grad(layer, inst, sums, at):
        base = W + half * PX

        def step(start, carry):
            rows = pl.multiple_of(base + start, W)
            g = grad_tile(layer, start, sums, at).astype(BF16)
            r.g3[inst, 1, pl.ds(rows, LANES), :] = g
            shifted(inst, rows, LANES, g.astype(F32))

        loop(4, LANES, step)
        for index, rows in ((0, grad_edge), (1, grad_rest)):
            piece = r.g3.at[inst, 1, rows, :]
            send(piece, piece, r.e_send.at[inst, index], r.e_recv.at[inst, index], beside)
            sent_later(piece, r.e_send.at[inst, index])

    def edge_ready(inst):
        arrived(r.g3.at[inst, 1, pl.ds(grad_edge_in, W), :], r.e_recv.at[inst, 0])
        shifted(
            inst, grad_edge_in, W, r.g3[inst, 1, pl.ds(grad_edge_in, W), :].astype(F32)
        )

    def rest_ready(inst):
        arrived(r.g3.at[inst, 1, pl.ds(grad_rest_in, PX - W), :], r.e_recv.at[inst, 1])

        def step(start, carry):
            rows = pl.multiple_of(grad_rest_in + start, W)
            shifted(inst, rows, 160, r.g3[inst, 1, pl.ds(rows, 160), :].astype(F32))

        loop(3, 160, step)

    def point_grad(layer, inst, sums, at):
        def step(start, carry):
            r.gp[inst, pl.ds(start, LANES), :] = grad_tile(layer, start, sums, at).astype(BF16)

        loop(4, LANES, step)

    def point_keep(inst, task, out):
        for j in range(4):
            rows = pl.ds(pl.multiple_of(lax.rem(j + core, 2) * LANES, LANES), LANES)
            r.mp[inst, j // 2, task, rows, :] = out[j * LANES : (j + 1) * LANES, :].astype(BF16)

    def point_exchange(inst):
        src = r.mp.at[inst, 1 - half]
        send(src, r.mr.at[inst], r.p_send.at[inst], r.p_recv.at[inst], beside)
        sent_later(src, r.p_send.at[inst])

    def point_sum(inst, piece):
        arrived(r.mr.at[inst], r.p_recv.at[inst])
        for task in range(TASKS):
            for side in range(2):
                for u in range(2):
                    rows = slice(side * LANES + u * 64, side * LANES + u * 64 + 64)
                    r.wg[2 * piece + u, side, task] = (
                        r.mp[inst, half, task, rows, :].astype(F32)
                        + r.mr[inst, task, rows, :].astype(F32)
                    ).astype(BF16)

    def windows(inst, start, rows):
        return [
            r.g3[inst, b, pl.ds(pl.multiple_of(start + (2 - a) * W, W), rows), :]
            for a in range(3)
            for b in range(3)
        ]

    def conv_terms(inst, weight):
        def terms(low, high):
            lhs = windows(inst, half * PX, PX)
            return lhs, [weight[tap, low:high, :] for tap in range(9)]

        return terms

    def point_terms(pairs):
        def terms(low, high):
            return (
                [r.gp[inst] for inst, _ in pairs],
                [weight[low:high, :] for _, weight in pairs],
            )

        return terms

    def slot_of(inst):
        return (0, 1, 2, 0, 1, 2, 3, 0)[inst]

    def scatter(inst, makers, blocks=(1, 0)):
        for block in blocks:
            lhs, rhs = [], []
            for maker in makers:
                more = maker(block * 256, block * 256 + 256)
                lhs += more[0]
                rhs += more[1]
            out = dot_nt(jnp.concatenate(lhs, axis=1), jnp.concatenate(rhs, axis=1))
            r.pf[slot_of(inst), block] = out[:, 0:LANES]
            r.ps[inst, block] = out[:, LANES:].astype(BF16)
            send(
                r.ps.at[inst, block],
                r.rr.at[inst, block],
                r.r_send.at[inst, block],
                r.r_recv.at[inst, block],
                mate,
            )
            sent_later(r.ps.at[inst, block], r.r_send.at[inst, block])

    def scatter_across(inst):
        arrived(r.rr.at[inst, 1], r.r_recv.at[inst, 1])

        def step(start, carry):
            rows = pl.ds(start, LANES)
            r.ps[inst, 2, rows, :] = (
                r.pf[slot_of(inst), 1, rows, :] + r.rr[inst, 1, rows, :].astype(F32)
            ).astype(BF16)

        loop(4, LANES, step)
        send(
            r.ps.at[inst, 2],
            r.rr.at[inst, 2],
            r.r_send.at[inst, 2],
            r.r_recv.at[inst, 2],
            across,
        )
        sent_later(r.ps.at[inst, 2], r.r_send.at[inst, 2])

    def scatter_done(inst):
        arrived(r.rr.at[inst, 0], r.r_recv.at[inst, 0])
        arrived(r.rr.at[inst, 2], r.r_recv.at[inst, 2])

    def scattered(inst, start):
        rows = pl.ds(start, LANES)
        return (
            r.pf[slot_of(inst), 0, rows, :]
            + r.rr[inst, 0, rows, :].astype(F32)
            + r.rr[inst, 2, rows, :].astype(F32)
        )

    def keep(piece, out):
        for side in range(2):
            for u in range(2):
                low = side * LANES + u * 64
                for b in range(3):
                    r.wg[2 * piece + u, side, b] = out[
                        low : low + 64, b * LANES : (b + 1) * LANES
                    ].astype(BF16)

    def conv_weights(turned, inst, first_chunk, a):
        rhs = jnp.concatenate(
            [r.g3[inst, b, (2 - a) * W : (2 - a) * W + IMAGE, :] for b in range(3)], axis=1
        )
        keep(first_chunk + a, dot(turned[...], rhs))

    def final(which, chunk, side):
        row = side * LANES + lax.rem(chunk, 2) * 64
        return r.fin.at[
            which, pl.ds(3 * lax.div(chunk, 2), 3), pl.ds(pl.multiple_of(row, 64), 64), :
        ]

    def service(chain, slot):
        first, counts, pause, doubling = CHAINS[chain]
        for side in range(2):
            place = image if side == 0 else images - 1 - image
            onward = d + 2 if side == 0 else d - 2
            step = slot - LAG * place
            chunk = first + step

            @pl.when((step >= 0) & (step < counts[side]))
            def _():
                @pl.when(place > 0)
                def _():
                    arrived(r.rx.at[chunk, side], r.c_recv.at[chunk, side])
                    summed = r.wg[chunk, side].astype(F32) + r.rx[chunk, side].astype(F32)

                    @pl.when(place < images - 1)
                    def _():
                        r.wg[chunk, side] = summed.astype(BF16)

                    @pl.when(place == images - 1)
                    def _():
                        final(0, chunk, side)[...] = summed.astype(BF16)

                        if doubling:

                            @pl.when(lax.rem(chunk, 4) == 3)
                            def _():
                                send(
                                    final(0, chunk, side),
                                    final(1, chunk, side),
                                    r.t_send.at[side],
                                    r.t_recv.at[chunk, side],
                                    beside,
                                )

                @pl.when(place < images - 1)
                def _():
                    send(
                        r.wg.at[chunk, side],
                        r.rx.at[chunk, side],
                        r.c_send.at[side],
                        r.c_recv.at[chunk, side],
                        (onward, t),
                    )

        for side in range(2):
            place = image if side == 0 else images - 1 - image
            back = d - 2 if side == 0 else d + 2
            step = slot - LAG * (images - 1) - pause - LAG * (images - 1 - place)
            chunk = first + step
            valid = (step >= 0) & (step < counts[side])
            single, both = valid, None
            if doubling:
                both = valid & (lax.rem(chunk, 4) == 3)
                single = valid & (lax.rem(chunk, 4) != 3)

            @pl.when(single)
            def _():
                mine = final(0, chunk, side)

                @pl.when(place < images - 1)
                def _():
                    arrived(mine, r.f_recv.at[chunk, side])

                @pl.when(place > 0)
                def _():
                    send(mine, mine, r.f_send.at[side], r.f_recv.at[chunk, side], (back, t))

                send(
                    mine,
                    final(1, chunk, side),
                    r.y_send.at[side],
                    r.y_recv.at[chain, side],
                    beside,
                )

            if not doubling:
                continue

            @pl.when(both)
            def _():
                two = final(slice(None), chunk, side)

                @pl.when(place < images - 1)
                def _():
                    arrived(two, r.f_recv.at[chunk, side])

                @pl.when(place == images - 1)
                def _():
                    arrived(final(1, chunk, side), r.t_recv.at[chunk, side])

                @pl.when(place > 0)
                def _():
                    send(two, two, r.f_send.at[side], r.f_recv.at[chunk, side], (back, t))

    progress = [0] * len(CHAINS)
    length = [max(counts) + 2 * LAG * (images - 1) + pause for _, counts, pause, _ in CHAINS]

    def advance(chain, count):
        low = progress[chain]
        progress[chain] = high = min(low + count, length[chain])
        if high == low + 1:
            service(chain, low)
        elif high > low:

            def one(slot, carry):
                service(chain, slot)
                return carry

            lax.fori_loop(low, high, one, 0)

    def advance_rest(chains):
        chains = [chain for chain in chains if progress[chain] < length[chain]]
        lows = [progress[chain] for chain in chains]

        def one(index, carry):
            for chain, low in zip(chains, lows):
                service(chain, low + index)
            return carry

        for chain in chains:
            progress[chain] = length[chain]
        if chains:
            count = max(length[chain] - low for chain, low in zip(chains, lows))
            lax.fori_loop(0, count, one, 0)

    ready = [0] * len(CHAINS)

    def units(count):
        return r.fin.at[0, 0:count, 0:192, :]

    def returned(chain):
        for side in range(2):
            arrived(units(CHAINS[chain][1][side] - BOTH[chain]), r.y_recv.at[chain, side])

    def mixed_grad(task):
        same, other = sums_recv(10 + task)
        store_layer_gains(MIXED + task, same, other, 0)
        conv_grad(MIXED + task, 3 + task, same, 0)

    def mixed_scatter(task, block):
        scatter(task, [conv_terms(3 + task, r.wt.at[pl.ds(9 * task, 9)])], (block,))

    def mixed_ready(task):
        rest_ready(3 + task)
        input_ready(r.vm.at[task], 3 + task)
        r.vt[2] = r.vm[task].T

    def mixed_weights(task, a):
        conv_weights(r.vt.at[2], 3 + task, 3 * task, a)
        ready[0] += 2

    def logit_slope(task):
        scatter_done(task)

        def step(start, carry):
            rows = pl.ds(start, LANES)
            masked = scattered(task, start)
            attention = r.att[task, rows, :]
            e = masked * r.h3[rows, :] * attention * (1.0 - attention)
            r.e[e_slot(LOGIT + task), rows, :] = e
            r.e[e_slot(THIRD), rows, :] = r.e[e_slot(THIRD), rows, :] + masked * attention
            return (carry[0] + fold(e * normed(LOGIT + task, start)), carry[1] + fold(e))

        sums = loop(4, LANES, step, (zeros8, zeros8))
        rows = [total(sums[0]), total(sums[1])]
        if task == 2:
            rows += slope_sums(THIRD, lambda start: r.e[e_slot(THIRD), pl.ds(start, LANES), :])
        sums_send(13 + task, rows)

    def logit_grad(task):
        same, other = sums_recv(13 + task)
        store_layer_gains(LOGIT + task, same, other, 0)
        if task == 2:
            store_layer_gains(THIRD, same, other, 1)
            conv_grad(THIRD, 2, same, 1)
        point_grad(LOGIT + task, task, same, 0)

    def logit_scatter(task):
        scatter(3 + task, [point_terms([(task, r.wu.at[task])])])

    def up_weights(task):
        point_keep(0, task, dot(r.xa[task], r.gp[task]))
        if task == 2:
            point_exchange(0)

    def turn_third():
        input_ready(r.v3, 2)
        r.vt[1] = r.v3[...].T

    def third_weights(a):
        conv_weights(r.vt.at[1], 2, 10, a)
        ready[1] += 2

    def up_sum():
        point_sum(0, 9)
        ready[1] += 2

    rows6 = []

    def project_slope(task):
        scatter_done(3 + task)
        rows6.extend(slope_sums(PROJ + task, functools.partial(scattered, 3 + task)))
        if task == 2:
            sums_send(16, rows6)

    def turn_one():
        flush(0)
        r.x2[W : W + PX, :] = r.x2[W : W + PX, :].T

    def second_slope():
        scatter_done(6)
        sums_send(17, slope_sums(SECOND, functools.partial(scattered, 6)))

    def project_grad():
        same, other = sums_recv(16)
        for task in range(TASKS):
            store_layer_gains(PROJ + task, same, other, task)
            point_grad(PROJ + task, 3 + task, same, task)

    def second_grad():
        same, other = sums_recv(17)
        store_layer_gains(SECOND, same, other, 0)
        conv_grad(SECOND, 1, same, 0)

    def down_weights():
        out = dot(r.x2[W : W + PX, :], jnp.concatenate([r.gp[3], r.gp[4], r.gp[5]], axis=1))
        for task in range(TASKS):
            point_keep(1, task, out[:, task * LANES : (task + 1) * LANES])
        point_exchange(1)

    def second_scatter(block):
        points = point_terms([(3 + task, r.wd.at[task]) for task in range(TASKS)])
        scatter(7, [conv_terms(1, r.w2), points], (block,))

    def second_weights(a):
        conv_weights(r.vt.at[0], 1, 14, a)
        ready[2] += 2

    def down_sum():
        point_sum(1, 13)
        ready[2] += 2

    def first_slope():
        scatter_done(7)
        sums_send(18, slope_sums(FIRST, functools.partial(scattered, 7)))

    def first_grad():
        same, other = sums_recv(18)
        store_layer_gains(FIRST, same, other, 0)
        conv_grad(FIRST, 0, same, 0)

    def first_weights():
        rest_ready(0)
        local_done(r.v1.at[my_image_rows, :], r.v_local.at[0])
        arrived(
            r.v1.at[pl.ds(pl.multiple_of((1 - half) * PX + (1 - core) * 256, 256), 256), :],
            r.v_recv.at[0, 1],
        )
        r.vt[2, 0:LANES, :] = r.v1[...].T
        for a in range(3):
            rhs = jnp.concatenate(
                [r.g3[0, b, pl.ds((2 - a) * W, IMAGE), :] for b in range(3)], axis=1
            )
            out = dot(r.vt[2, 0:LANES, :], rhs)
            for b in range(3):
                for u in range(2):
                    r.wg[2 * (17 + a // 2) + u, a % 2, b] = out[
                        u * 64 : u * 64 + 64, b * LANES : (b + 1) * LANES
                    ].astype(BF16)
        ready[3] += 4

    def features_back():
        lhs = jnp.concatenate(windows(0, half * PX, PX), axis=1)
        out = dot_nt(lhs, jnp.concatenate([r.w1[tap] for tap in range(9)], axis=1))
        r.ff[...] = out[:, 0:LANES]
        r.fs[0] = out[:, LANES:].astype(BF16)
        send(r.fs.at[0], r.fr.at[0], r.feat_send.at[4], r.feat_recv.at[4], across)
        sent_later(r.fs.at[0], r.feat_send.at[4])

    def features_sum():
        arrived(r.fr.at[0], r.feat_recv.at[4])

        def step(start, carry):
            rows = pl.ds(start, LANES)
            both = r.ff[rows, :] + r.fr[0, rows, :].astype(F32)
            r.ff[rows, :] = both
            r.fs[1, rows, :] = both.astype(BF16)

        loop(4, LANES, step)
        send(r.fs.at[1], r.fr.at[1], r.feat_send.at[5], r.feat_recv.at[5], mate)
        sent_later(r.fs.at[1], r.feat_send.at[5])

    def features_store():
        arrived(r.fr.at[1], r.feat_recv.at[5])

        def step(start, carry):
            rows = pl.ds(start, LANES)
            both = r.ff[rows, :] + r.fr[1, rows, :].astype(F32)
            turned = jnp.where(core == 0, both, pltpu.roll(both, LANES // 2, 1))
            r.b_fg[rows, :] = turned[:, 0 : LANES // 2].astype(BF16)

        loop(4, LANES, step)
        emit(r.b_fg, r.ofg, 2)
        emit(r.b_gb, r.ogb, 3)

    def chain_step(chain):
        whole = ready[chain] == max(CHAINS[chain][1])
        if progress[chain] < (length[chain] if whole else ready[chain] * (chain == 0)):
            advance(chain, 1)

    def third_scatter(block):
        scatter(6, [conv_terms(2, r.w3)], (block,))

    third_own()
    activated_out()
    third_forward()
    third_far()
    forward_input(r.v2, 1)
    gather_forward(r.xa.at[0], 2, 0)
    turn_second()
    logits(0)
    gather_forward(r.xa.at[1], 3, 0)
    activate()
    gather_forward(r.xa.at[2], 4, 0)
    attend(0)
    logits(1)
    logits(2)
    shared_pool()
    attend(1)
    mixed_own(0)
    mixed_forward(0)
    attend(2)
    mixed_own(1)
    mixed_far(0)
    mixed_forward(1)
    mixed_own(2)
    forward_input(r.v3, 2)
    mixed_slope(0)
    mixed_far(1)
    mixed_forward(2)
    mixed_grad(0)
    mixed_far(2)
    mixed_slope(1)
    edge_ready(3)
    chain_step(2)
    forward_input(r.vm.at[0], 3)
    mixed_scatter(0, 1)
    forward_input(r.vm.at[1], 4)
    chain_step(3)
    mixed_scatter(0, 0)
    mixed_slope(2)
    chain_step(3)
    mixed_grad(1)
    mixed_ready(0)
    mixed_weights(0, 0)
    mixed_weights(0, 1)
    mixed_weights(0, 2)
    chain_step(0)
    chain_step(0)
    chain_step(3)
    chain_step(1)
    chain_step(2)
    chain_step(2)
    edge_ready(4)
    forward_input(r.vm.at[2], 5)
    chain_step(2)
    chain_step(1)
    mixed_grad(2)
    scatter_across(0)
    mixed_scatter(1, 0)
    mixed_scatter(1, 1)
    chain_step(0)
    mixed_ready(1)
    chain_step(2)
    chain_step(0)
    mixed_weights(1, 0)
    mixed_weights(1, 1)
    chain_step(1)
    scatter_across(1)
    edge_ready(5)
    chain_step(0)
    logit_slope(0)
    chain_step(1)
    chain_step(1)
    chain_step(0)
    mixed_scatter(2, 1)
    chain_step(2)
    mixed_weights(1, 2)
    mixed_scatter(2, 0)
    chain_step(1)
    logit_slope(1)
    chain_step(0)
    chain_step(0)
    scatter_across(2)
    chain_step(3)
    chain_step(1)
    chain_step(3)
    chain_step(3)
    mixed_ready(2)
    mixed_weights(2, 0)
    mixed_weights(2, 1)
    chain_step(0)
    logit_slope(2)
    chain_step(0)
    chain_step(3)
    chain_step(3)
    chain_step(2)
    mixed_weights(2, 2)
    turn_activated(1)
    logit_grad(0)
    chain_step(3)
    logit_scatter(0)
    chain_step(3)
    chain_step(2)
    chain_step(0)
    turn_activated(0)
    chain_step(1)
    chain_step(1)
    chain_step(3)
    turn_third()
    chain_step(0)
    logit_grad(1)
    scatter_across(3)
    chain_step(0)
    chain_step(2)
    logit_grad(2)
    up_weights(0)
    chain_step(1)
    logit_scatter(1)
    turn_activated(2)
    chain_step(2)
    chain_step(0)
    edge_ready(2)
    chain_step(1)
    chain_step(1)
    chain_step(1)
    third_scatter(0)
    chain_step(3)
    chain_step(0)
    third_scatter(1)
    chain_step(2)
    chain_step(2)
    mixed_pool(2)
    scatter_across(4)
    logit_scatter(2)
    chain_step(2)
    chain_step(1)
    chain_step(0)
    chain_step(2)
    chain_step(1)
    scatter_across(6)
    chain_step(1)
    chain_step(3)
    chain_step(0)
    mixed_pool(1)
    chain_step(3)
    chain_step(2)
    chain_step(3)
    scatter_across(5)
    up_weights(1)
    chain_step(2)
    chain_step(2)
    mixed_pool(0)
    chain_step(2)
    chain_step(0)
    chain_step(1)
    up_weights(2)
    chain_step(3)
    rest_ready(2)
    chain_step(2)
    third_weights(0)
    third_weights(1)
    third_weights(2)
    chain_step(1)
    second_slope()
    chain_step(0)
    project_slope(0)
    emit(r.b_tp, r.otp, 1)
    chain_step(1)
    up_sum()
    chain_step(3)
    chain_step(0)
    chain_step(2)
    chain_step(1)
    turn_one()
    project_slope(1)
    project_slope(2)
    chain_step(0)
    chain_step(2)
    chain_step(1)
    chain_step(1)
    second_grad()
    chain_step(1)
    chain_step(0)
    project_grad()
    chain_step(0)
    chain_step(1)
    chain_step(3)
    down_weights()
    chain_step(1)
    chain_step(0)
    chain_step(2)
    edge_ready(1)
    second_scatter(1)
    chain_step(0)
    chain_step(2)
    chain_step(1)
    second_scatter(0)
    rest_ready(1)
    second_weights(0)
    second_weights(1)
    second_weights(2)
    scatter_across(7)
    down_sum()
    chain_step(2)
    chain_step(0)
    chain_step(1)
    chain_step(2)
    chain_step(0)
    chain_step(3)
    chain_step(1)
    first_slope()
    chain_step(2)
    chain_step(1)
    chain_step(0)
    chain_step(1)
    chain_step(0)
    chain_step(2)
    chain_step(0)
    chain_step(1)
    chain_step(2)
    first_grad()
    chain_step(1)
    chain_step(0)
    chain_step(0)
    chain_step(3)
    chain_step(3)
    chain_step(1)
    edge_ready(0)
    features_back()
    chain_step(2)
    chain_step(1)
    chain_step(2)
    chain_step(0)
    chain_step(1)
    features_sum()
    chain_step(1)
    chain_step(2)
    chain_step(2)
    first_weights()
    chain_step(1)
    chain_step(0)
    features_store()
    chain_step(3)
    chain_step(2)
    chain_step(0)

    advance_rest([0])
    for key in list(pending):
        flush(key)
    advance_rest([3, 1, 2])
    for chain in range(len(CHAINS)):
        returned(chain)

    for side in range(2):
        place = image if side == 0 else images - 1 - image
        single = CHUNKS[side] - sum(BOTH)

        @pl.when(place < images - 1)
        def _():
            left(units(CHUNKS[side]), r.c_send.at[side])

        @pl.when(place == images - 1)
        def _():
            left(units(sum(BOTH)), r.t_send.at[side])

        @pl.when(place > 0)
        def _():
            left(units(single + 2 * sum(BOTH)), r.f_send.at[side])

        left(units(single), r.y_send.at[side])


def step_kernel(dp_size, operands):
    anywhere = pl.BlockSpec(memory_space=pl.ANY)
    in_names = ["feat", "dom", "k1", "k2", "k3", "kt", "md", "mu"]
    in_names += ["sg", "sb", "tg", "tb", "sct", "tct"]
    scalars = pl.BlockSpec(memory_space=pltpu.SMEM)
    in_specs = [anywhere, scalars] + [anywhere] * 12
    outs = dict(
        osp=((PX // 4, LANES), BF16, anywhere),
        otp=((TASKS, PX // 4, LANES), BF16, anywhere),
        ofg=((PX, LANES // 2), BF16, anywhere),
        ogb=((48, LANES), F32, anywhere),
        fin=((2, 3 * PIECES, 256, LANES), BF16, pl.BlockSpec(memory_space=pltpu.VMEM)),
    )
    tall, deep = PX + 2 * W, IMAGE + 2 * W
    scratch = dict(
        b_sct=((PX // 4, LANES), BF16),
        b_tct=((TASKS, PX // 4, LANES), BF16),
        b_sg=((3, DOMAINS, LANES), F32),
        b_sb=((3, DOMAINS, LANES), F32),
        b_tg=((9, DOMAINS, LANES), F32),
        b_tb=((9, DOMAINS, LANES), F32),
        b_sp=((PX // 4, LANES), BF16),
        b_tp=((TASKS, PX // 4, LANES), BF16),
        b_fg=((PX, LANES // 2), BF16),
        b_gb=((48, LANES), F32),
        w1=((9, 256, LANES), BF16),
        w2=((9, 512, LANES), BF16),
        w3=((9, 512, LANES), BF16),
        wt=((27, 512, LANES), BF16),
        wd=((3, 512, LANES), BF16),
        wu=((3, 512, LANES), BF16),
        x1=((tall, 256), BF16),
        x2=((tall, 512), BF16),
        x3=((tall, 512), BF16),
        xm=((TASKS, tall, 512), BF16),
        xa=((TASKS, PX, 512), BF16),
        v1=((IMAGE, LANES), BF16),
        v2=((IMAGE, 256), BF16),
        v3=((IMAGE, 256), BF16),
        vm=((TASKS, IMAGE, 256), BF16),
        vt=((3, 256, IMAGE), BF16),
        acc=((2, PX, 3 * LANES), F32),
        fm=((4, PX, LANES // 2), BF16),
        fh=((4, W, LANES // 2), BF16),
        same=((-(-dp_size // 8) * 8, LANES), F32),
        pre=((12, PX, LANES), F32),
        e=((7, PX, LANES), F32),
        bn=((12, 8, LANES), F32),
        h3=((PX, LANES), F32),
        ht=((TASKS, PX, LANES), F32),
        att=((TASKS, PX, LANES), F32),
        g3=((6, 3, deep, LANES), BF16),
        gp=((6, PX, LANES), BF16),
        mp=((2, 2, TASKS, 256, LANES), BF16),
        mr=((2, TASKS, 256, LANES), BF16),
        pf=((4, 2, PX, LANES), F32),
        ps=((8, 3, PX, LANES), BF16),
        rr=((8, 3, PX, LANES), BF16),
        ff=((PX, LANES), F32),
        fs=((2, PX, LANES), BF16),
        fr=((2, PX, LANES), BF16),
        st=((ROUNDS, 2, LANES), F32),
        sr=((ROUNDS, dp_size - 1, 2, LANES), F32),
        st8=((len(WIDE), 8, LANES), F32),
        sr8=((len(WIDE), dp_size - 1, 8, LANES), F32),
        wg=((CHUNKS[0], 2, 3, 64, LANES), BF16),
        rx=((CHUNKS[0], 2, 3, 64, LANES), BF16),
    )
    sems = dict(
        weight_sem=(7,),
        small_sem=(6,),
        emit_sem=(4,),
        feat_send=(6,),
        feat_recv=(6,),
        g_send=(8, 4),
        g_recv=(8, 5),
        v_send=(6, 2),
        v_recv=(6, 2),
        v_local=(6,),
        st_send=(ROUNDS,),
        st_recv=(ROUNDS,),
        e_send=(6, 2),
        e_recv=(6, 2),
        p_send=(2,),
        p_recv=(2,),
        r_send=(8, 3),
        r_recv=(8, 3),
        c_send=(2,),
        c_recv=(CHUNKS[0], 2),
        t_send=(2,),
        t_recv=(CHUNKS[0], 2),
        f_send=(2,),
        f_recv=(CHUNKS[0], 2),
        y_send=(2,),
        y_recv=(4, 2),
    )
    names = in_names + list(outs) + list(scratch) + list(sems)
    return pl.pallas_call(
        functools.partial(kernel, dp_size, names),
        out_shape=[
            (pltpu.VMEM if name == "fin" else jax.ShapeDtypeStruct)(shape, kind)
            for name, (shape, kind, _) in outs.items()
        ],
        in_specs=in_specs,
        out_specs=[spec for _, _, spec in outs.values()],
        scratch_shapes=[pltpu.VMEM(shape, kind) for shape, kind in scratch.values()]
        + [pltpu.SemaphoreType.DMA(shape) for shape in sems.values()],
        compiler_params=pltpu.CompilerParams(
            collective_id=0, has_side_effects=True, vmem_limit_bytes=54 * 1024 * 1024
        ),
        cost_estimate=pl.CostEstimate(
            flops=11_000_000_000, bytes_accessed=16_000_000, transcendentals=12_000_000
        ),
    )(*operands)


def finish_kernel(
    shared, tasks, back, gains, finals,
    o_shared, o_tasks, o_back, o_first, o_second, o_third, o_gain, o_bias, o_down, o_up, o_conv,
    o_tgain, o_tbias,
    wide, table, gain, bias, tgain, tbias, in_sem, out_sem,
):
    copies = []

    def write(src, dst):
        copy = pltpu.make_async_copy(src, dst, out_sem.at[len(copies)])
        copy.start()
        copies.append(copy)

    rows = pltpu.make_async_copy(gains, table, in_sem)
    rows.start()
    for src, dst in ((shared, o_shared), (tasks, o_tasks), (back, o_back)):
        write(src, dst)
    rows.wait()
    for target, out, base, count in (
        (gain, o_gain, 0, 3),
        (bias, o_bias, 6, 3),
        (tgain, o_tgain, 12, 9),
        (tbias, o_tbias, 30, 9),
    ):
        for row in range(count):
            target[row] = table[base + 2 * row : base + 2 * row + 2, :]
        write(target, out)
    targets = [(o_conv, 3 * piece) for piece in range(9)]
    targets += [(o_up, 0)] + [(o_third, 3 * a) for a in range(3)]
    targets += [(o_down, 0)] + [(o_second, 3 * a) for a in range(3)]
    pair = lax.div(lax.axis_index("tensor"), 2)
    half = lax.rem(lax.axis_index("dp"), 2)
    spots = [
        pl.multiple_of(lax.rem(pair + which, 2) * 256, 256) for which in (half, 1 - half)
    ]
    for piece in range(PIECES):

        def widen(plane, carry, piece=piece):
            for index, spot in enumerate(spots):
                wide[piece, plane, pl.ds(spot, 256), :] = finals[index, 3 * piece + plane].astype(F32)
            return carry

        lax.fori_loop(0, 3, widen, 0)
        if piece < 17:
            target, plane = targets[piece]
            write(wide.at[piece], target.at[plane : plane + 3])
            continue
        for side in range(2 if piece == 17 else 1):
            for block in range(2):
                low = 256 * block + LANES * side
                tap = 3 * side if piece == 17 else 6
                write(
                    wide.at[piece, :, low : low + LANES, :],
                    o_first.at[tap : tap + 3, LANES * block : LANES * (block + 1), :],
                )
    for copy in copies:
        copy.wait()


def finish(shared, tasks, back, gains, weights):
    anywhere = pl.BlockSpec(memory_space=pl.ANY)

    def array(shape, like):
        return jax.ShapeDtypeStruct(shape, like)

    return pl.pallas_call(
        finish_kernel,
        out_shape=[
            array(shared.shape, BF16),
            array(tasks.shape, BF16),
            array(back.shape, BF16),
            array((9, 256, LANES), F32),
            array((9, 512, LANES), F32),
            array((9, 512, LANES), F32),
            array((3, DOMAINS, LANES), F32),
            array((3, DOMAINS, LANES), F32),
            array((3, 512, LANES), F32),
            array((3, 512, LANES), F32),
            array((27, 512, LANES), F32),
            array((9, DOMAINS, LANES), F32),
            array((9, DOMAINS, LANES), F32),
        ],
        in_specs=[anywhere] * 4 + [pl.BlockSpec(memory_space=pltpu.VMEM)],
        out_specs=[anywhere] * 13,
        scratch_shapes=[
            pltpu.VMEM((PIECES, 3, 512, LANES), F32),
            pltpu.VMEM((48, LANES), F32),
            pltpu.VMEM((3, DOMAINS, LANES), F32),
            pltpu.VMEM((3, DOMAINS, LANES), F32),
            pltpu.VMEM((9, DOMAINS, LANES), F32),
            pltpu.VMEM((9, DOMAINS, LANES), F32),
            pltpu.SemaphoreType.DMA,
            pltpu.SemaphoreType.DMA((30,)),
        ],
        compiler_params=pltpu.CompilerParams(vmem_limit_bytes=54 * 1024 * 1024),
        cost_estimate=pl.CostEstimate(flops=0, bytes_accessed=23_000_000, transcendentals=0),
    )(shared, tasks, back, gains, pltpu.with_memory_space_constraint(weights, pltpu.VMEM))


def body(
    features,
    domain_index,
    conv_first,
    conv_second,
    conv_third,
    shared_gain,
    shared_bias,
    mask_down,
    mask_up,
    task_conv,
    task_gain,
    task_bias,
    shared_cotangent,
    task_cotangent,
):
    dp_size = lax.axis_size("dp")
    narrow = features.shape[2]
    shared, tasks, back, gains, weights = step_kernel(
        dp_size,
        (
            features.reshape(PX, narrow),
            domain_index,
            conv_first.reshape(9, 256, LANES),
            conv_second.reshape(9, 512, LANES),
            conv_third.reshape(9, 512, LANES),
            task_conv.reshape(27, 512, LANES),
            mask_down,
            mask_up,
            shared_gain,
            shared_bias,
            task_gain.reshape(9, DOMAINS, LANES),
            task_bias.reshape(9, DOMAINS, LANES),
            shared_cotangent.reshape(PX // 4, LANES),
            task_cotangent.reshape(TASKS, PX // 4, LANES),
        ),
    )
    shared, tasks, back, first, second, third, gain, bias, down, up, conv, tgain, tbias = finish(
        shared, tasks, back, gains, weights
    )
    return (
        shared.reshape(ROWS // 2, W // 2, LANES),
        tasks.reshape(TASKS, ROWS // 2, W // 2, LANES),
        back.reshape(features.shape),
        first.reshape(3, 3, 256, LANES),
        second.reshape(3, 3, 512, LANES),
        third.reshape(3, 3, 512, LANES),
        gain,
        bias,
        down,
        up,
        conv.reshape(TASKS, 3, 3, 512, LANES),
        tgain.reshape(3, TASKS, DOMAINS, LANES),
        tbias.reshape(3, TASKS, DOMAINS, LANES),
    )


def solution(mesh):
    return jax.shard_map(
        body,
        mesh=mesh,
        in_specs=(
            P("dp", None, "tensor"),
            P(),
            P(None, None, None, "tensor"),
            P(None, None, None, "tensor"),
            P(None, None, None, "tensor"),
            P(None, None, "tensor"),
            P(None, None, "tensor"),
            P(None, None, "tensor"),
            P(None, None, "tensor"),
            P(None, None, None, None, "tensor"),
            P(None, None, None, "tensor"),
            P(None, None, None, "tensor"),
            P("dp", None, "tensor"),
            P(None, "dp", None, "tensor"),
        ),
        out_specs=(
            P("dp", None, "tensor"),
            P(None, "dp", None, "tensor"),
            P("dp", None, "tensor"),
            P(None, None, None, "tensor"),
            P(None, None, None, "tensor"),
            P(None, None, None, "tensor"),
            P(None, None, "tensor"),
            P(None, None, "tensor"),
            P(None, None, "tensor"),
            P(None, None, "tensor"),
            P(None, None, None, None, "tensor"),
            P(None, None, None, "tensor"),
            P(None, None, None, "tensor"),
        ),
        check_vma=False,
    )
```

profile of v0, /device:TPU:0, one launch (start us, length us, event | category | flops | bytes accessed | tf_op | source)
XLA Modules:
  0.0 197.7 jit_solution(10961711495864862287)
XLA Ops:
  0.7 187.5 %shard_map.237 = (bf16[128,128]{1,0:T(8,128)(2,1)}, bf16[3,128,128]{2,1,0:T(8,128)(2,1)}, bf16[512,64]{1,0:T(8,128)(2,1)}, f32[48,128]{1,0:T(8,128)}, bf16[2,57,256,128]{3,2,1,0:T(8,128)(2,1)S(1)}) custom-call(bf16[512,64]{1,0:T(8,128)(2,1)} %bitcast.26, s32[4]{0:T(128)} %refs_1_.1, bf16[9,256,128]{2,1,0:T(8,128)(2,1)} %bitcast.25, ...), custom_call_target="tpu_custom_call" | custom-call | flops 11000000512 | bytes 16000000 | tf_op jit(solution)/shard_map/pallas_call | solution.py:1495
  188.2 9.4 %shard_map.238 = (bf16[128,128]{1,0:T(8,128)(2,1)}, bf16[3,128,128]{2,1,0:T(8,128)(2,1)}, bf16[512,64]{1,0:T(8,128)(2,1)}, f32[9,256,128]{2,1,0:T(8,128)}, f32[9...) custom-call(bf16[128,128]{1,0:T(8,128)(2,1)} %get-tuple-element.31.s, ...), custom_call_target="tpu_custom_call" | custom-call | bytes 23000000 | tf_op jit(solution)/shard_map/pallas_call | solution.py:1579
where the time goes:
time: 198 us
  Pallas kernels  197 us (99%)
    pallas_call x1, Pallas kernels, step_kernel(): pl.pallas_call(functools.partial(kernel, dp_size, names), out_shape=[(plt...  188 us
    pallas_call x1, Pallas kernels, finish(): pl.pallas_call(finish_kernel, out_shape=[array(shared.shape, BF16), array...  9.37 us

commit v1 on v0

--- a/solution.py
+++ b/solution.py
@@ -25,7 +25,11 @@
     (26, (8, 8), 2, True),
     (34, (4, 2), 0, False),
 )
-BOTH = (4, 2, 2, 0)
+DOUBLE = 4
+BOTH = tuple(
+    sum(chunk * DOUBLE % 16 < DOUBLE for chunk in range(first, first + counts[0])) * doubling
+    for first, counts, _, doubling in CHAINS
+)
 LAG = 2
 ROUNDS = 19
 WIDE = (2, 15, 16)
@@ -186,16 +190,6 @@
             r.w1.at[:, j * LANES : (j + 1) * LANES, :],
             r.weight_sem.at[5],
         )
-    for index, (source, target) in enumerate(
-        ((r.k2, r.w2), (r.k3, r.w3), (r.kt, r.wt), (r.md, r.wd), (r.mu, r.wu))
-    ):
-        for j in range(4):
-            rows = pl.ds(pl.multiple_of(peers[j] * LANES, LANES), LANES)
-            local(
-                source.at[:, rows, :],
-                target.at[:, j * LANES : (j + 1) * LANES, :],
-                r.weight_sem.at[index],
-            )
     pl.semaphore_wait(barrier, dp_size - 1 + 6)
 
     own_rows = pl.ds(W, PX)
@@ -220,6 +214,17 @@
     for j in (2, 3, 1):
         send(r.feat, r.fm.at[j], r.feat_send.at[j], r.feat_recv.at[j], (d, peers[j]))
         sent_later(r.fm.at[j], r.feat_send.at[j])
+
+    for index, (source, target) in enumerate(
+        ((r.k2, r.w2), (r.md, r.wd), (r.k3, r.w3), (r.mu, r.wu), (r.kt, r.wt))
+    ):
+        for j in range(4):
+            rows = pl.ds(pl.multiple_of(peers[j] * LANES, LANES), LANES)
+            local(
+                source.at[:, rows, :],
+                target.at[:, j * LANES : (j + 1) * LANES, :],
+                r.weight_sem.at[index],
+            )
 
     def unpool(ct, target):
         def step(start, carry):
@@ -481,17 +486,13 @@
     )
     sent_later(piece, r.v_send.at[0, 0])
     sums_send(0, conv(r.x1, r.w1, FIRST, LANES, r.acc.at[0]))
-    local_done(r.w2, r.weight_sem.at[0])
-    local_done(r.w3, r.weight_sem.at[1])
-    local_done(r.wt, r.weight_sem.at[2])
-    local_done(r.wd, r.weight_sem.at[3])
-    local_done(r.wu, r.weight_sem.at[4])
     for index in range(2, 6):
         local_done(small[index][1], r.small_sem.at[index])
     same = sums_same(0)
     norm_setup(FIRST, same, 0)
     silu_to(FIRST, r.x2, W)
     gather(r.x2, 0, True, W)
+    local_done(r.w2, r.weight_sem.at[0])
     gather_near(r.x2, 0, True, W)
     conv_own(r.x2, r.w2, 256, r.acc.at[0])
     gather_forward(r.x2, 0, W)
@@ -505,6 +506,7 @@
 
     sums_send(1, conv(r.x2, r.w2, SECOND, 256, r.acc.at[0]))
 
+    local_done(r.wd, r.weight_sem.at[1])
     taps = jnp.concatenate([r.wd[task] for task in range(TASKS)], axis=1)
     out = dot(r.x2[W : W + PX, :], taps)
     for task in range(TASKS):
@@ -522,12 +524,14 @@
         norm_setup(PROJ + task, same, task)
         silu_to(PROJ + task, r.xa.at[task], 0)
     def third_own():
+        local_done(r.w3, r.weight_sem.at[2])
+        local_done(r.wu, r.weight_sem.at[3])
+        local_done(r.wt, r.weight_sem.at[4])
         gather_near(r.x3, 1, True, W)
         conv_own(r.x3, r.w3, 256, r.acc.at[0])
 
-    def activated_out():
-        for task in range(TASKS):
-            gather(r.xa.at[task], 2 + task, False, 0)
+    def activated_out(task):
+        gather(r.xa.at[task], 2 + task, False, 0)
 
     def third_forward():
         gather_forward(r.x3, 1, W)
@@ -806,10 +810,7 @@
         keep(first_chunk + a, dot(turned[...], rhs))
 
     def final(which, chunk, side):
-        row = side * LANES + lax.rem(chunk, 2) * 64
-        return r.fin.at[
-            which, pl.ds(3 * lax.div(chunk, 2), 3), pl.ds(pl.multiple_of(row, 64), 64), :
-        ]
+        return r.fin.at[chunk, side, which]
 
     def service(chain, slot):
         first, counts, pause, doubling = CHAINS[chain]
@@ -836,7 +837,7 @@
 
                         if doubling:
 
-                            @pl.when(lax.rem(chunk, 4) == 3)
+                            @pl.when(lax.rem(chunk * DOUBLE, 16) < DOUBLE)
                             def _():
                                 send(
                                     final(0, chunk, side),
@@ -864,8 +865,8 @@
             valid = (step >= 0) & (step < counts[side])
             single, both = valid, None
             if doubling:
-                both = valid & (lax.rem(chunk, 4) == 3)
-                single = valid & (lax.rem(chunk, 4) != 3)
+                double = lax.rem(chunk * DOUBLE, 16) < DOUBLE
+                both, single = valid & double, valid & jnp.logical_not(double)
 
             @pl.when(single)
             def _():
@@ -877,7 +878,7 @@
 
                 @pl.when(place > 0)
                 def _():
-                    send(mine, mine, r.f_send.at[side], r.f_recv.at[chunk, side], (back, t))
+                    send(mine, mine, r.f_send.at[0, side], r.f_recv.at[chunk, side], (back, t))
 
                 send(
                     mine,
@@ -892,7 +893,7 @@
 
             @pl.when(both)
             def _():
-                two = final(slice(None), chunk, side)
+                two = r.fin.at[chunk, side]
 
                 @pl.when(place < images - 1)
                 def _():
@@ -904,7 +905,7 @@
 
                 @pl.when(place > 0)
                 def _():
-                    send(two, two, r.f_send.at[side], r.f_recv.at[chunk, side], (back, t))
+                    send(two, two, r.f_send.at[1, side], r.f_recv.at[chunk, side], (back, t))
 
     progress = [0] * len(CHAINS)
     length = [max(counts) + 2 * LAG * (images - 1) + pause for _, counts, pause, _ in CHAINS]
@@ -940,7 +941,7 @@
     ready = [0] * len(CHAINS)
 
     def units(count):
-        return r.fin.at[0, 0:count, 0:192, :]
+        return r.fin.at[0:count, 0, 0]
 
     def returned(chain):
         for side in range(2):
@@ -1125,248 +1126,235 @@
     def third_scatter(block):
         scatter(6, [conv_terms(2, r.w3)], (block,))
 
+    chain_step(1)
+    activated_out(0)
     third_own()
-    activated_out()
+    activated_out(1)
     third_forward()
+    activated_out(2)
+    gather_forward(r.xa.at[0], 2, 0)
     third_far()
     forward_input(r.v2, 1)
-    gather_forward(r.xa.at[0], 2, 0)
-    turn_second()
     logits(0)
     gather_forward(r.xa.at[1], 3, 0)
+    turn_second()
     activate()
     gather_forward(r.xa.at[2], 4, 0)
     attend(0)
     logits(1)
+    shared_pool()
     logits(2)
-    shared_pool()
     attend(1)
     mixed_own(0)
     mixed_forward(0)
+    chain_step(0)
     attend(2)
     mixed_own(1)
     mixed_far(0)
     mixed_forward(1)
     mixed_own(2)
-    forward_input(r.v3, 2)
     mixed_slope(0)
     mixed_far(1)
     mixed_forward(2)
     mixed_grad(0)
+    forward_input(r.v3, 2)
     mixed_far(2)
+    chain_step(1)
+    chain_step(0)
     mixed_slope(1)
     edge_ready(3)
-    chain_step(2)
+    mixed_scatter(0, 1)
+    chain_step(1)
     forward_input(r.vm.at[0], 3)
-    mixed_scatter(0, 1)
-    forward_input(r.vm.at[1], 4)
-    chain_step(3)
     mixed_scatter(0, 0)
     mixed_slope(2)
-    chain_step(3)
     mixed_grad(1)
+    scatter_across(0)
     mixed_ready(0)
+    forward_input(r.vm.at[1], 4)
     mixed_weights(0, 0)
+    chain_step(0)
     mixed_weights(0, 1)
     mixed_weights(0, 2)
-    chain_step(0)
-    chain_step(0)
-    chain_step(3)
-    chain_step(1)
-    chain_step(2)
-    chain_step(2)
     edge_ready(4)
     forward_input(r.vm.at[2], 5)
-    chain_step(2)
-    chain_step(1)
+    chain_step(0)
+    chain_step(1)
+    chain_step(1)
+    mixed_scatter(1, 1)
+    chain_step(0)
     mixed_grad(2)
-    scatter_across(0)
+    chain_step(1)
     mixed_scatter(1, 0)
-    mixed_scatter(1, 1)
-    chain_step(0)
     mixed_ready(1)
-    chain_step(2)
-    chain_step(0)
     mixed_weights(1, 0)
+    chain_step(0)
     mixed_weights(1, 1)
-    chain_step(1)
     scatter_across(1)
+    chain_step(1)
+    chain_step(0)
+    chain_step(3)
     edge_ready(5)
-    chain_step(0)
     logit_slope(0)
-    chain_step(1)
-    chain_step(1)
-    chain_step(0)
     mixed_scatter(2, 1)
-    chain_step(2)
+    chain_step(0)
     mixed_weights(1, 2)
+    chain_step(2)
+    chain_step(0)
     mixed_scatter(2, 0)
-    chain_step(1)
     logit_slope(1)
-    chain_step(0)
-    chain_step(0)
     scatter_across(2)
-    chain_step(3)
-    chain_step(1)
-    chain_step(3)
-    chain_step(3)
+    chain_step(0)
+    chain_step(2)
+    chain_step(1)
     mixed_ready(2)
     mixed_weights(2, 0)
+    chain_step(2)
+    chain_step(0)
     mixed_weights(2, 1)
     chain_step(0)
     logit_slope(2)
-    chain_step(0)
     chain_step(3)
-    chain_step(3)
-    chain_step(2)
-    mixed_weights(2, 2)
+    chain_step(1)
     turn_activated(1)
     logit_grad(0)
+    chain_step(0)
+    logit_scatter(0)
+    chain_step(0)
+    turn_activated(0)
+    mixed_weights(2, 2)
+    turn_third()
+    logit_grad(1)
+    chain_step(0)
+    chain_step(2)
+    scatter_across(3)
+    chain_step(2)
+    logit_grad(2)
+    logit_scatter(1)
+    chain_step(2)
+    chain_step(2)
+    chain_step(0)
+    turn_activated(2)
     chain_step(3)
-    logit_scatter(0)
+    up_weights(0)
+    chain_step(0)
+    edge_ready(2)
     chain_step(3)
-    chain_step(2)
-    chain_step(0)
-    turn_activated(0)
-    chain_step(1)
-    chain_step(1)
-    chain_step(3)
-    turn_third()
-    chain_step(0)
-    logit_grad(1)
-    scatter_across(3)
-    chain_step(0)
-    chain_step(2)
-    logit_grad(2)
-    up_weights(0)
-    chain_step(1)
-    logit_scatter(1)
-    turn_activated(2)
-    chain_step(2)
-    chain_step(0)
-    edge_ready(2)
-    chain_step(1)
-    chain_step(1)
-    chain_step(1)
+    scatter_across(4)
     third_scatter(0)
     chain_step(3)
-    chain_step(0)
+    chain_step(2)
     third_scatter(1)
-    chain_step(2)
+    logit_scatter(2)
+    chain_step(2)
+    mixed_pool(1)
+    chain_step(0)
+    chain_step(1)
+    up_weights(1)
+    scatter_across(6)
+    chain_step(2)
+    chain_step(0)
+    scatter_across(5)
+    chain_step(1)
+    chain_step(2)
+    chain_step(0)
     chain_step(2)
     mixed_pool(2)
-    scatter_across(4)
-    logit_scatter(2)
-    chain_step(2)
-    chain_step(1)
-    chain_step(0)
-    chain_step(2)
-    chain_step(1)
-    scatter_across(6)
-    chain_step(1)
-    chain_step(3)
-    chain_step(0)
-    mixed_pool(1)
-    chain_step(3)
-    chain_step(2)
-    chain_step(3)
-    scatter_across(5)
-    up_weights(1)
-    chain_step(2)
-    chain_step(2)
-    mixed_pool(0)
-    chain_step(2)
-    chain_step(0)
-    chain_step(1)
+    rest_ready(2)
     up_weights(2)
-    chain_step(3)
-    rest_ready(2)
     chain_step(2)
     third_weights(0)
+    chain_step(1)
     third_weights(1)
     third_weights(2)
-    chain_step(1)
+    chain_step(2)
+    chain_step(2)
+    mixed_pool(0)
+    chain_step(1)
+    project_slope(0)
     second_slope()
-    chain_step(0)
-    project_slope(0)
+    chain_step(2)
+    chain_step(0)
     emit(r.b_tp, r.otp, 1)
-    chain_step(1)
+    chain_step(3)
+    chain_step(2)
     up_sum()
-    chain_step(3)
-    chain_step(0)
-    chain_step(2)
-    chain_step(1)
+    chain_step(1)
+    chain_step(2)
+    chain_step(0)
     turn_one()
     project_slope(1)
+    chain_step(3)
     project_slope(2)
-    chain_step(0)
-    chain_step(2)
+    chain_step(2)
+    chain_step(0)
     chain_step(1)
     chain_step(1)
     second_grad()
     chain_step(1)
+    chain_step(1)
+    chain_step(3)
     chain_step(0)
     project_grad()
-    chain_step(0)
-    chain_step(1)
+    edge_ready(1)
+    rest_ready(1)
+    chain_step(0)
+    chain_step(1)
+    down_weights()
+    chain_step(1)
+    second_scatter(0)
+    chain_step(2)
+    chain_step(0)
     chain_step(3)
-    down_weights()
-    chain_step(1)
-    chain_step(0)
-    chain_step(2)
-    edge_ready(1)
     second_scatter(1)
     chain_step(0)
-    chain_step(2)
-    chain_step(1)
-    second_scatter(0)
-    rest_ready(1)
     second_weights(0)
     second_weights(1)
+    chain_step(1)
     second_weights(2)
     scatter_across(7)
     down_sum()
     chain_step(2)
     chain_step(0)
-    chain_step(1)
-    chain_step(2)
-    chain_step(0)
-    chain_step(3)
-    chain_step(1)
-    first_slope()
-    chain_step(2)
-    chain_step(1)
-    chain_step(0)
-    chain_step(1)
-    chain_step(0)
-    chain_step(2)
-    chain_step(0)
-    chain_step(1)
-    chain_step(2)
-    first_grad()
-    chain_step(1)
-    chain_step(0)
-    chain_step(0)
+    chain_step(2)
+    chain_step(1)
+    chain_step(0)
+    chain_step(2)
     chain_step(3)
     chain_step(3)
+    first_slope()
+    chain_step(1)
+    chain_step(1)
+    chain_step(0)
+    chain_step(0)
+    chain_step(1)
+    chain_step(1)
+    first_grad()
+    chain_step(2)
+    chain_step(2)
+    chain_step(0)
+    chain_step(1)
     chain_step(1)
     edge_ready(0)
     features_back()
     chain_step(2)
-    chain_step(1)
-    chain_step(2)
-    chain_step(0)
-    chain_step(1)
+    chain_step(2)
+    chain_step(1)
+    chain_step(3)
+    chain_step(0)
     features_sum()
     chain_step(1)
     chain_step(2)
     chain_step(2)
+    chain_step(1)
     first_weights()
-    chain_step(1)
-    chain_step(0)
     features_store()
     chain_step(3)
-    chain_step(2)
+    chain_step(1)
+    chain_step(3)
+    chain_step(2)
+    chain_step(0)
+    chain_step(1)
     chain_step(0)
 
     advance_rest([0])
@@ -1390,7 +1378,8 @@
 
         @pl.when(place > 0)
         def _():
-            left(units(single + 2 * sum(BOTH)), r.f_send.at[side])
+            left(units(single), r.f_send.at[0, side])
+            left(r.fin.at[0 : sum(BOTH), 0], r.f_send.at[1, side])
 
         left(units(single), r.y_send.at[side])
 
@@ -1406,7 +1395,7 @@
         otp=((TASKS, PX // 4, LANES), BF16, anywhere),
         ofg=((PX, LANES // 2), BF16, anywhere),
         ogb=((48, LANES), F32, anywhere),
-        fin=((2, 3 * PIECES, 256, LANES), BF16, pl.BlockSpec(memory_space=pltpu.VMEM)),
+        fin=((CHUNKS[0], 2, 2, 3, 64, LANES), BF16, pl.BlockSpec(memory_space=pltpu.VMEM)),
     )
     tall, deep = PX + 2 * W, IMAGE + 2 * W
     scratch = dict(
@@ -1486,7 +1475,7 @@
         c_recv=(CHUNKS[0], 2),
         t_send=(2,),
         t_recv=(CHUNKS[0], 2),
-        f_send=(2,),
+        f_send=(2, 2),
         f_recv=(CHUNKS[0], 2),
         y_send=(2,),
         y_recv=(4, 2),
@@ -1550,7 +1539,11 @@
 
         def widen(plane, carry, piece=piece):
             for index, spot in enumerate(spots):
-                wide[piece, plane, pl.ds(spot, 256), :] = finals[index, 3 * piece + plane].astype(F32)
+                for side in range(2):
+                    for u in range(2):
+                        rows = pl.ds(pl.multiple_of(spot + side * LANES + u * 64, 64), 64)
+                        part = finals[2 * piece + u, side, index, plane]
+                        wide[piece, plane, rows, :] = part.astype(F32)
             return carry
 
         lax.fori_loop(0, 3, widen, 0)

time: 198 us -> 195 us (0.985)
  Pallas kernels: 197 us -> 194 us
    pallas_call x1, Pallas kernels: 188 us -> 185 us  [step_kernel(): pl.pallas_call(functools.partial(kernel, dp_size, names), out_shape=[(plt...]
where the time goes in v1:
time: 195 us
  Pallas kernels  194 us (99%)
    pallas_call x1, Pallas kernels, step_kernel(): pl.pallas_call(functools.partial(kernel, dp_size, names), out_shape=[(plt...  185 us
    pallas_call x1, Pallas kernels, finish(): pl.pallas_call(finish_kernel, out_shape=[array(shared.shape, BF16), array...  9.37 us

profile of v1, /device:TPU:0, one launch (start us, length us, event | category | flops | bytes accessed | tf_op | source)
XLA Modules:
  0.0 195.0 jit_solution(11719021896442734261)
XLA Ops:
  0.7 184.8 %shard_map.237 = (bf16[128,128]{1,0:T(8,128)(2,1)}, bf16[3,128,128]{2,1,0:T(8,128)(2,1)}, bf16[512,64]{1,0:T(8,128)(2,1)}, f32[48,128]{1,0:T(8,128)}, bf16[38,2,2,3,64,128]{5,4,3,2,1,0:T(8,128)(2,1)S(1)}) custom-call(bf16[512,64]{1,0:T(8,128)(2,1)} %bitcast.26, s32[4]{0:T(128)} %refs_1_.1, bf16[9,256,128]{2,1,0:T(8,128)(2,1)} %bitcast.25, ...), custom_call_target="tpu_custom_call" | custom-call | flops 11000000512 | bytes 16000000 | tf_op jit(solution)/shard_map/pallas_call | solution.py:1484
  185.5 9.4 %shard_map.238 = (bf16[128,128]{1,0:T(8,128)(2,1)}, bf16[3,128,128]{2,1,0:T(8,128)(2,1)}, bf16[512,64]{1,0:T(8,128)(2,1)}, f32[9,256,128]{2,1,0:T(8,128)}, f32[9...) custom-call(bf16[128,128]{1,0:T(8,128)(2,1)} %get-tuple-element.31.s, ...), custom_call_target="tpu_custom_call" | custom-call | bytes 23000000 | tf_op jit(solution)/shard_map/pallas_call | solution.py:1572

commit v2 on v1

--- a/solution.py
+++ b/solution.py
@@ -25,10 +25,10 @@
     (26, (8, 8), 2, True),
     (34, (4, 2), 0, False),
 )
-DOUBLE = 4
+DOUBLE = (4, 4, 4, 0)
 BOTH = tuple(
-    sum(chunk * DOUBLE % 16 < DOUBLE for chunk in range(first, first + counts[0])) * doubling
-    for first, counts, _, doubling in CHAINS
+    sum(step * share % 16 < share for step in range(counts[1]))
+    for share, (_, counts, _, _) in zip(DOUBLE, CHAINS)
 )
 LAG = 2
 ROUNDS = 19
@@ -535,7 +535,6 @@
 
     def third_forward():
         gather_forward(r.x3, 1, W)
-        exchange_input(r.x3, r.v3, 2, W)
 
     def third_far():
         gather_far(r.x3, 1, True, W)
@@ -592,6 +591,8 @@
 
     def mixed_forward(task):
         gather_forward(r.xm.at[task], 5 + task, W)
+
+    def mixed_exchange(task):
         exchange_input(r.xm.at[task], r.vm.at[task], 3 + task, W)
 
     def mixed_far(task):
@@ -814,6 +815,7 @@
 
     def service(chain, slot):
         first, counts, pause, doubling = CHAINS[chain]
+        share = DOUBLE[chain]
         for side in range(2):
             place = image if side == 0 else images - 1 - image
             onward = d + 2 if side == 0 else d - 2
@@ -837,7 +839,7 @@
 
                         if doubling:
 
-                            @pl.when(lax.rem(chunk * DOUBLE, 16) < DOUBLE)
+                            @pl.when(lax.rem(step * share, 16) < share)
                             def _():
                                 send(
                                     final(0, chunk, side),
@@ -865,7 +867,7 @@
             valid = (step >= 0) & (step < counts[side])
             single, both = valid, None
             if doubling:
-                double = lax.rem(chunk * DOUBLE, 16) < DOUBLE
+                double = lax.rem(step * share, 16) < share
                 both, single = valid & double, valid & jnp.logical_not(double)
 
             @pl.when(single)
@@ -957,6 +959,8 @@
 
     def mixed_ready(task):
         rest_ready(3 + task)
+
+    def turn_masked(task):
         input_ready(r.vm.at[task], 3 + task)
         r.vt[2] = r.vm[task].T
 
@@ -1010,11 +1014,12 @@
         point_sum(0, 9)
         ready[1] += 2
 
-    rows6 = []
+    rows6 = [None] * 6
 
     def project_slope(task):
         scatter_done(3 + task)
-        rows6.extend(slope_sums(PROJ + task, functools.partial(scattered, 3 + task)))
+        sums = slope_sums(PROJ + task, functools.partial(scattered, 3 + task))
+        rows6[2 * task : 2 * task + 2] = sums
         if task == 2:
             sums_send(16, rows6)
 
@@ -1126,11 +1131,11 @@
     def third_scatter(block):
         scatter(6, [conv_terms(2, r.w3)], (block,))
 
-    chain_step(1)
     activated_out(0)
     third_own()
     activated_out(1)
     third_forward()
+    exchange_input(r.x3, r.v3, 2, W)
     activated_out(2)
     gather_forward(r.xa.at[0], 2, 0)
     third_far()
@@ -1147,215 +1152,210 @@
     attend(1)
     mixed_own(0)
     mixed_forward(0)
-    chain_step(0)
+    mixed_exchange(0)
     attend(2)
     mixed_own(1)
     mixed_far(0)
     mixed_forward(1)
+    mixed_exchange(1)
     mixed_own(2)
+    forward_input(r.v3, 2)
     mixed_slope(0)
     mixed_far(1)
     mixed_forward(2)
+    mixed_exchange(2)
+    chain_step(3)
+    forward_input(r.vm.at[1], 4)
     mixed_grad(0)
-    forward_input(r.v3, 2)
     mixed_far(2)
-    chain_step(1)
-    chain_step(0)
     mixed_slope(1)
     edge_ready(3)
     mixed_scatter(0, 1)
-    chain_step(1)
     forward_input(r.vm.at[0], 3)
     mixed_scatter(0, 0)
     mixed_slope(2)
     mixed_grad(1)
+    chain_step(1)
     scatter_across(0)
+    forward_input(r.vm.at[2], 5)
+    turn_masked(0)
     mixed_ready(0)
-    forward_input(r.vm.at[1], 4)
     mixed_weights(0, 0)
     chain_step(0)
     mixed_weights(0, 1)
+    edge_ready(4)
+    chain_step(0)
     mixed_weights(0, 2)
-    edge_ready(4)
-    forward_input(r.vm.at[2], 5)
-    chain_step(0)
-    chain_step(1)
-    chain_step(1)
     mixed_scatter(1, 1)
     chain_step(0)
     mixed_grad(2)
-    chain_step(1)
     mixed_scatter(1, 0)
+    chain_step(1)
+    chain_step(0)
     mixed_ready(1)
+    turn_masked(1)
+    chain_step(2)
+    chain_step(2)
+    chain_step(0)
+    logit_slope(0)
     mixed_weights(1, 0)
-    chain_step(0)
+    chain_step(1)
+    chain_step(2)
     mixed_weights(1, 1)
     scatter_across(1)
-    chain_step(1)
+    chain_step(2)
+    edge_ready(5)
+    chain_step(2)
+    chain_step(0)
+    mixed_scatter(2, 1)
+    chain_step(2)
+    chain_step(2)
+    chain_step(0)
+    mixed_scatter(2, 0)
+    chain_step(2)
+    mixed_weights(1, 2)
+    chain_step(0)
+    scatter_across(2)
+    chain_step(0)
+    mixed_ready(2)
+    logit_slope(1)
+    turn_masked(2)
+    mixed_weights(2, 0)
     chain_step(0)
     chain_step(3)
-    edge_ready(5)
-    logit_slope(0)
-    mixed_scatter(2, 1)
-    chain_step(0)
-    mixed_weights(1, 2)
-    chain_step(2)
-    chain_step(0)
-    mixed_scatter(2, 0)
-    logit_slope(1)
-    scatter_across(2)
-    chain_step(0)
-    chain_step(2)
-    chain_step(1)
-    mixed_ready(2)
-    mixed_weights(2, 0)
-    chain_step(2)
-    chain_step(0)
+    logit_slope(2)
+    logit_grad(0)
+    chain_step(1)
+    chain_step(1)
+    turn_activated(1)
+    chain_step(0)
+    logit_scatter(0)
     mixed_weights(2, 1)
     chain_step(0)
-    logit_slope(2)
+    turn_activated(0)
+    logit_grad(1)
+    chain_step(2)
+    turn_third()
+    chain_step(0)
     chain_step(3)
-    chain_step(1)
-    turn_activated(1)
-    logit_grad(0)
-    chain_step(0)
-    logit_scatter(0)
-    chain_step(0)
-    turn_activated(0)
+    scatter_across(3)
+    logit_grad(2)
+    up_weights(0)
+    logit_scatter(1)
+    chain_step(0)
     mixed_weights(2, 2)
-    turn_third()
-    logit_grad(1)
-    chain_step(0)
-    chain_step(2)
-    scatter_across(3)
-    chain_step(2)
-    logit_grad(2)
-    logit_scatter(1)
-    chain_step(2)
-    chain_step(2)
-    chain_step(0)
     turn_activated(2)
-    chain_step(3)
-    up_weights(0)
+    chain_step(1)
     chain_step(0)
     edge_ready(2)
     chain_step(3)
+    third_scatter(1)
     scatter_across(4)
     third_scatter(0)
+    logit_scatter(2)
+    mixed_pool(1)
+    chain_step(2)
+    chain_step(0)
+    up_weights(1)
+    chain_step(1)
+    scatter_across(6)
+    chain_step(2)
+    chain_step(2)
+    chain_step(0)
+    scatter_across(5)
+    rest_ready(2)
+    mixed_pool(0)
+    mixed_pool(2)
+    chain_step(0)
+    chain_step(1)
+    up_weights(2)
+    project_slope(1)
+    third_weights(0)
+    project_slope(0)
+    chain_step(1)
     chain_step(3)
-    chain_step(2)
-    third_scatter(1)
-    logit_scatter(2)
-    chain_step(2)
-    mixed_pool(1)
-    chain_step(0)
-    chain_step(1)
-    up_weights(1)
-    scatter_across(6)
-    chain_step(2)
-    chain_step(0)
-    scatter_across(5)
-    chain_step(1)
-    chain_step(2)
-    chain_step(0)
-    chain_step(2)
-    mixed_pool(2)
-    rest_ready(2)
-    up_weights(2)
-    chain_step(2)
-    third_weights(0)
-    chain_step(1)
     third_weights(1)
+    chain_step(2)
+    chain_step(1)
     third_weights(2)
-    chain_step(2)
-    chain_step(2)
-    mixed_pool(0)
-    chain_step(1)
-    project_slope(0)
     second_slope()
-    chain_step(2)
-    chain_step(0)
+    chain_step(3)
+    chain_step(0)
+    up_sum()
+    chain_step(1)
+    chain_step(0)
+    project_slope(2)
+    turn_one()
     emit(r.b_tp, r.otp, 1)
-    chain_step(3)
-    chain_step(2)
-    up_sum()
-    chain_step(1)
-    chain_step(2)
-    chain_step(0)
-    turn_one()
-    project_slope(1)
-    chain_step(3)
-    project_slope(2)
-    chain_step(2)
     chain_step(0)
     chain_step(1)
     chain_step(1)
     second_grad()
     chain_step(1)
     chain_step(1)
-    chain_step(3)
     chain_step(0)
     project_grad()
+    chain_step(1)
     edge_ready(1)
     rest_ready(1)
     chain_step(0)
     chain_step(1)
+    second_weights(0)
     down_weights()
-    chain_step(1)
+    chain_step(2)
+    chain_step(0)
     second_scatter(0)
-    chain_step(2)
-    chain_step(0)
-    chain_step(3)
     second_scatter(1)
-    chain_step(0)
-    second_weights(0)
     second_weights(1)
-    chain_step(1)
+    chain_step(0)
+    chain_step(0)
+    chain_step(2)
     second_weights(2)
+    chain_step(1)
+    chain_step(2)
     scatter_across(7)
     down_sum()
     chain_step(2)
     chain_step(0)
-    chain_step(2)
-    chain_step(1)
-    chain_step(0)
-    chain_step(2)
+    chain_step(1)
+    chain_step(2)
+    first_slope()
+    chain_step(1)
+    chain_step(0)
+    chain_step(1)
+    chain_step(0)
     chain_step(3)
     chain_step(3)
-    first_slope()
-    chain_step(1)
-    chain_step(1)
-    chain_step(0)
-    chain_step(0)
-    chain_step(1)
-    chain_step(1)
+    chain_step(0)
+    chain_step(0)
+    chain_step(3)
+    chain_step(2)
+    chain_step(1)
+    chain_step(1)
+    chain_step(2)
+    chain_step(2)
     first_grad()
     chain_step(2)
-    chain_step(2)
-    chain_step(0)
-    chain_step(1)
     chain_step(1)
     edge_ready(0)
     features_back()
-    chain_step(2)
+    chain_step(1)
     chain_step(2)
     chain_step(1)
     chain_step(3)
-    chain_step(0)
     features_sum()
-    chain_step(1)
-    chain_step(2)
-    chain_step(2)
-    chain_step(1)
+    chain_step(0)
+    chain_step(2)
+    chain_step(1)
+    chain_step(0)
     first_weights()
+    chain_step(3)
+    chain_step(2)
+    chain_step(1)
+    chain_step(1)
     features_store()
+    chain_step(2)
     chain_step(3)
-    chain_step(1)
-    chain_step(3)
-    chain_step(2)
-    chain_step(0)
-    chain_step(1)
-    chain_step(0)
 
     advance_rest([0])
     for key in list(pending):

time: 195 us -> 198 us (1.015)
  Pallas kernels: 194 us -> 197 us
    pallas_call x1, Pallas kernels: 185 us -> 188 us  [step_kernel(): pl.pallas_call(functools.partial(kernel, dp_size, names), out_shape=[(plt...]
where the time goes in v2:
time: 198 us
  Pallas kernels  197 us (99%)
    pallas_call x1, Pallas kernels, step_kernel(): pl.pallas_call(functools.partial(kernel, dp_size, names), out_shape=[(plt...  188 us
    pallas_call x1, Pallas kernels, finish(): pl.pallas_call(finish_kernel, out_shape=[array(shared.shape, BF16), array...  9.37 us

profile of v2, /device:TPU:0, one launch (start us, length us, event | category | flops | bytes accessed | tf_op | source)
XLA Modules:
  0.0 198.0 jit_solution(16127676537646408486)
XLA Ops:
  0.7 187.8 %shard_map.237 = (bf16[128,128]{1,0:T(8,128)(2,1)}, bf16[3,128,128]{2,1,0:T(8,128)(2,1)}, bf16[512,64]{1,0:T(8,128)(2,1)}, f32[48,128]{1,0:T(8,128)}, bf16[38,2,2,3,64,128]{5,4,3,2,1,0:T(8,128)(2,1)S(1)}) custom-call(bf16[512,64]{1,0:T(8,128)(2,1)} %bitcast.26, s32[4]{0:T(128)} %refs_1_.1, bf16[9,256,128]{2,1,0:T(8,128)(2,1)} %bitcast.25, ...), custom_call_target="tpu_custom_call" | custom-call | flops 11000000512 | bytes 16000000 | tf_op jit(solution)/shard_map/pallas_call | solution.py:1484
  188.4 9.4 %shard_map.238 = (bf16[128,128]{1,0:T(8,128)(2,1)}, bf16[3,128,128]{2,1,0:T(8,128)(2,1)}, bf16[512,64]{1,0:T(8,128)(2,1)}, f32[9,256,128]{2,1,0:T(8,128)}, f32[9...) custom-call(bf16[128,128]{1,0:T(8,128)(2,1)} %get-tuple-element.31.s, ...), custom_call_target="tpu_custom_call" | custom-call | bytes 23000000 | tf_op jit(solution)/shard_map/pallas_call | solution.py:1572

commit v3 on v1

--- a/solution.py
+++ b/solution.py
@@ -1010,11 +1010,12 @@
         point_sum(0, 9)
         ready[1] += 2
 
-    rows6 = []
+    rows6 = [None] * 6
 
     def project_slope(task):
         scatter_done(3 + task)
-        rows6.extend(slope_sums(PROJ + task, functools.partial(scattered, 3 + task)))
+        sums = slope_sums(PROJ + task, functools.partial(scattered, 3 + task))
+        rows6[2 * task : 2 * task + 2] = sums
         if task == 2:
             sums_send(16, rows6)
 
@@ -1126,15 +1127,15 @@
     def third_scatter(block):
         scatter(6, [conv_terms(2, r.w3)], (block,))
 
-    chain_step(1)
     activated_out(0)
+    forward_input(r.v2, 1)
     third_own()
     activated_out(1)
     third_forward()
     activated_out(2)
     gather_forward(r.xa.at[0], 2, 0)
     third_far()
-    forward_input(r.v2, 1)
+    chain_step(1)
     logits(0)
     gather_forward(r.xa.at[1], 3, 0)
     turn_second()
@@ -1143,11 +1144,11 @@
     attend(0)
     logits(1)
     shared_pool()
+    chain_step(0)
     logits(2)
     attend(1)
     mixed_own(0)
     mixed_forward(0)
-    chain_step(0)
     attend(2)
     mixed_own(1)
     mixed_far(0)
@@ -1158,47 +1159,50 @@
     mixed_forward(2)
     mixed_grad(0)
     forward_input(r.v3, 2)
+    forward_input(r.vm.at[1], 4)
+    chain_step(0)
     mixed_far(2)
-    chain_step(1)
-    chain_step(0)
     mixed_slope(1)
     edge_ready(3)
     mixed_scatter(0, 1)
-    chain_step(1)
     forward_input(r.vm.at[0], 3)
     mixed_scatter(0, 0)
     mixed_slope(2)
+    chain_step(0)
     mixed_grad(1)
     scatter_across(0)
     mixed_ready(0)
-    forward_input(r.vm.at[1], 4)
     mixed_weights(0, 0)
     chain_step(0)
     mixed_weights(0, 1)
     mixed_weights(0, 2)
     edge_ready(4)
+    chain_step(1)
+    chain_step(2)
     forward_input(r.vm.at[2], 5)
-    chain_step(0)
-    chain_step(1)
-    chain_step(1)
+    mixed_grad(2)
+    chain_step(0)
     mixed_scatter(1, 1)
     chain_step(0)
-    mixed_grad(2)
-    chain_step(1)
+    chain_step(1)
+    chain_step(2)
     mixed_scatter(1, 0)
     mixed_ready(1)
+    chain_step(0)
     mixed_weights(1, 0)
+    chain_step(3)
     chain_step(0)
     mixed_weights(1, 1)
+    chain_step(1)
     scatter_across(1)
-    chain_step(1)
-    chain_step(0)
-    chain_step(3)
+    chain_step(0)
+    chain_step(1)
     edge_ready(5)
     logit_slope(0)
     mixed_scatter(2, 1)
     chain_step(0)
     mixed_weights(1, 2)
+    chain_step(1)
     chain_step(2)
     chain_step(0)
     mixed_scatter(2, 0)
@@ -1206,110 +1210,105 @@
     scatter_across(2)
     chain_step(0)
     chain_step(2)
-    chain_step(1)
     mixed_ready(2)
+    chain_step(2)
+    chain_step(3)
+    chain_step(0)
     mixed_weights(2, 0)
-    chain_step(2)
-    chain_step(0)
+    chain_step(0)
+    turn_third()
     mixed_weights(2, 1)
-    chain_step(0)
     logit_slope(2)
-    chain_step(3)
     chain_step(1)
     turn_activated(1)
     logit_grad(0)
     chain_step(0)
+    chain_step(2)
+    chain_step(2)
+    chain_step(2)
     logit_scatter(0)
     chain_step(0)
     turn_activated(0)
+    chain_step(2)
     mixed_weights(2, 2)
-    turn_third()
+    chain_step(2)
     logit_grad(1)
     chain_step(0)
-    chain_step(2)
     scatter_across(3)
-    chain_step(2)
     logit_grad(2)
     logit_scatter(1)
-    chain_step(2)
-    chain_step(2)
     chain_step(0)
     turn_activated(2)
+    up_weights(0)
+    chain_step(0)
     chain_step(3)
-    up_weights(0)
-    chain_step(0)
     edge_ready(2)
-    chain_step(3)
+    mixed_pool(1)
     scatter_across(4)
     third_scatter(0)
     chain_step(3)
     chain_step(2)
     third_scatter(1)
     logit_scatter(2)
-    chain_step(2)
-    mixed_pool(1)
-    chain_step(0)
-    chain_step(1)
+    chain_step(0)
     up_weights(1)
     scatter_across(6)
-    chain_step(2)
     chain_step(0)
     scatter_across(5)
     chain_step(1)
-    chain_step(2)
-    chain_step(0)
-    chain_step(2)
+    chain_step(0)
+    project_slope(0)
     mixed_pool(2)
     rest_ready(2)
+    chain_step(3)
     up_weights(2)
-    chain_step(2)
     third_weights(0)
     chain_step(1)
     third_weights(1)
+    chain_step(2)
+    chain_step(2)
     third_weights(2)
     chain_step(2)
     chain_step(2)
+    chain_step(2)
     mixed_pool(0)
-    chain_step(1)
-    project_slope(0)
     second_slope()
-    chain_step(2)
     chain_step(0)
     emit(r.b_tp, r.otp, 1)
-    chain_step(3)
-    chain_step(2)
+    turn_one()
     up_sum()
     chain_step(1)
     chain_step(2)
     chain_step(0)
-    turn_one()
+    chain_step(2)
     project_slope(1)
-    chain_step(3)
     project_slope(2)
-    chain_step(2)
     chain_step(0)
     chain_step(1)
     chain_step(1)
     second_grad()
     chain_step(1)
-    chain_step(1)
-    chain_step(3)
     chain_step(0)
     project_grad()
     edge_ready(1)
     rest_ready(1)
-    chain_step(0)
-    chain_step(1)
+    chain_step(2)
+    chain_step(0)
+    chain_step(1)
+    chain_step(2)
+    chain_step(3)
     down_weights()
     chain_step(1)
     second_scatter(0)
-    chain_step(2)
     chain_step(0)
     chain_step(3)
     second_scatter(1)
     chain_step(0)
+    chain_step(1)
     second_weights(0)
     second_weights(1)
+    chain_step(3)
+    chain_step(0)
     chain_step(1)
     second_weights(2)
     scatter_across(7)
@@ -1317,44 +1316,45 @@
     chain_step(2)
     chain_step(0)
     chain_step(2)
-    chain_step(1)
-    chain_step(0)
-    chain_step(2)
+    chain_step(2)
+    chain_step(1)
     chain_step(3)
+    chain_step(0)
+    chain_step(2)
     chain_step(3)
     first_slope()
     chain_step(1)
     chain_step(1)
-    chain_step(0)
+    chain_step(1)
+    chain_step(0)
+    chain_step(2)
     chain_step(0)
     chain_step(1)
     chain_step(1)
     first_grad()
     chain_step(2)
     chain_step(2)
-    chain_step(0)
-    chain_step(1)
-    chain_step(1)
+    chain_step(1)
+    chain_step(0)
+    chain_step(0)
     edge_ready(0)
     features_back()
-    chain_step(2)
-    chain_step(2)
-    chain_step(1)
+    chain_step(0)
+    chain_step(2)
+    chain_step(1)
+    chain_step(0)
+    first_weights()
+    features_sum()
     chain_step(3)
-    chain_step(0)
-    features_sum()
-    chain_step(1)
-    chain_step(2)
-    chain_step(2)
-    chain_step(1)
-    first_weights()
+    chain_step(2)
+    chain_step(1)
+    chain_step(3)
+    chain_step(2)
+    chain_step(1)
+    chain_step(1)
     features_store()
     chain_step(3)
-    chain_step(1)
-    chain_step(3)
-    chain_step(2)
-    chain_step(0)
-    chain_step(1)
+    chain_step(0)
     chain_step(0)
 
     advance_rest([0])

time: 195 us -> 196 us (level)
  no operation moved by 1% of the time
where the time goes in v3:
time: 196 us
  Pallas kernels  195 us (99%)
    pallas_call x1, Pallas kernels, step_kernel(): pl.pallas_call(functools.partial(kernel, dp_size, names), out_shape=[(plt...  186 us
    pallas_call x1, Pallas kernels, finish(): pl.pallas_call(finish_kernel, out_shape=[array(shared.shape, BF16), array...  9.37 us

profile of v3, /device:TPU:0, one launch (start us, length us, event | category | flops | bytes accessed | tf_op | source)
XLA Modules:
  0.0 195.8 jit_solution(8459454876071036341)
XLA Ops:
  0.7 185.6 %shard_map.237 = (bf16[128,128]{1,0:T(8,128)(2,1)}, bf16[3,128,128]{2,1,0:T(8,128)(2,1)}, bf16[512,64]{1,0:T(8,128)(2,1)}, f32[48,128]{1,0:T(8,128)}, bf16[38,2,2,3,64,128]{5,4,3,2,1,0:T(8,128)(2,1)S(1)}) custom-call(bf16[512,64]{1,0:T(8,128)(2,1)} %bitcast.26, s32[4]{0:T(128)} %refs_1_.1, bf16[9,256,128]{2,1,0:T(8,128)(2,1)} %bitcast.25, ...), custom_call_target="tpu_custom_call" | custom-call | flops 11000000512 | bytes 16000000 | tf_op jit(solution)/shard_map/pallas_call | solution.py:1484
  186.2 9.4 %shard_map.238 = (bf16[128,128]{1,0:T(8,128)(2,1)}, bf16[3,128,128]{2,1,0:T(8,128)(2,1)}, bf16[512,64]{1,0:T(8,128)(2,1)}, f32[9,256,128]{2,1,0:T(8,128)}, f32[9...) custom-call(bf16[128,128]{1,0:T(8,128)(2,1)} %get-tuple-element.31.s, ...), custom_call_target="tpu_custom_call" | custom-call | bytes 23000000 | tf_op jit(solution)/shard_map/pallas_call | solution.py:1572
